TPU v7x, 512 devices: a whole 4x4x16 slice. The times are simulated.
512 devices in a mesh: pipe: 4 (over y), seq: 16 (over z), tensor: 8 (over x, core).
Axes of the slice: x: 4, y: 4, z: 16, core: 2. Of those that a mesh axis runs over, the one named last changes fastest.
Arguments:
- layer_input: bfloat16 [4, 2048, 8192], P('pipe', 'seq', 'tensor'), may hold values from -320 to 320
- conv_out: bfloat16 [4, 2048, 8192], P('pipe', 'seq', 'tensor'), may hold values from -8 to 8
- act_grad: bfloat16 [4, 2048, 8192], P('pipe', 'seq', 'tensor'), may hold values from -6 to 6
- conv_kernel: bfloat16 [4, 4, 8192], P('pipe', None, 'tensor'), may hold values from -3 to 3
- in_proj: bfloat16 [4, 8192, 8192], P('pipe', 'seq', 'tensor'), may hold values from -0.0625 to 0.0625
- sketch_matrix: bfloat16 [4, 8192, 512], P('pipe', 'tensor'), may hold values from -0.0625 to 0.0625
Outputs:
- passed_grad: bfloat16 [4, 2048, 8192], P('pipe', 'tensor', 'seq')
- basis: bfloat16 [4, 8192, 512], P('pipe', 'tensor')
All inputs are finite; a program needn't handle non-finite values.
Results may differ from a plain program's by a relative error of at most 0.017.
Values may be sent and summed in bfloat16 or wider, within the bound.
No kernel may reach another device: no remote copies, remote signals or barrier semaphores. Data moves between devices by JAX's collectives and lax.ppermute only.
A program may use at most 64 MiB of HBM per device.

v0:
```python
import math

import jax
import jax.numpy as jnp
from jax import lax
from jax.sharding import PartitionSpec as P

D = 8192


def passed_along(block, axis, distance):
    devices = range(lax.axis_size(axis))
    route = [(i - distance, i) for i in devices if i - distance in devices]
    return lax.ppermute(block, axis, route)


def shifted(value, axis, by):
    count = lax.axis_size(axis)
    return lax.ppermute(value, axis, [(i, (i + by) % count) for i in range(count)])


def finish_basis(sketch, gram):
    low = jnp.linalg.cholesky(gram)
    ortho_t = lax.linalg.triangular_solve(low, sketch.T, left_side=True, lower=True)
    return (ortho_t.T * math.sqrt(D)).astype(jnp.bfloat16)


def local(layer_input, conv_out, act_grad, conv_kernel, in_proj, sketch_matrix):
    acts = layer_input[0]
    kernel = conv_kernel[0]
    weights = in_proj[0]
    test_matrix = sketch_matrix[0]
    tok_rows = acts.shape[0]
    taps = kernel.shape[0]
    pval = conv_out[0].astype(jnp.float32)
    sig = jax.nn.sigmoid(pval)
    pre_grad = act_grad[0].astype(jnp.float32) * sig * (1.0 + pval * (1.0 - sig))
    ahead = passed_along(pre_grad[: taps - 1], "seq", -1)
    extended = jnp.concatenate([pre_grad, ahead], axis=0)
    total = jnp.zeros(pre_grad.shape, jnp.float32)
    for tap in range(taps):
        total = total + kernel[tap].astype(jnp.float32) * extended[tap : tap + tok_rows]
    in_grad = total.astype(jnp.bfloat16)
    partial_grad = lax.dot_general(
        lax.all_gather(in_grad, "seq", axis=0, tiled=True),
        weights,
        (((1,), (1,)), ((), ())),
        preferred_element_type=jnp.float32,
    )
    input_grad = lax.psum_scatter(
        partial_grad.astype(jnp.bfloat16), "tensor", scatter_dimension=0, tiled=True
    )
    passed = shifted(input_grad, "pipe", -1)
    row_terms = jnp.dot(in_grad, test_matrix, preferred_element_type=jnp.float32)
    sketch_rows = lax.psum(row_terms, "tensor").astype(jnp.bfloat16)
    sketch_part = lax.dot_general(
        acts, sketch_rows, (((0,), (0,)), ((), ())), preferred_element_type=jnp.float32
    )
    sketch = lax.psum(sketch_part, "seq")
    gram_part = jnp.dot(sketch.T, sketch, precision=lax.Precision.HIGHEST)
    gram = lax.psum(gram_part, "tensor")
    basis = finish_basis(sketch, gram)
    return (passed[None], basis[None])


def solution(mesh):
    placed = (
        P("pipe", "seq", "tensor"),
        P("pipe", "seq", "tensor"),
        P("pipe", "seq", "tensor"),
        P("pipe", None, "tensor"),
        P("pipe", "seq", "tensor"),
        P("pipe", "tensor", None),
    )
    return jax.shard_map(
        local,
        mesh=mesh,
        in_specs=placed,
        out_specs=(P("pipe", "tensor", "seq"), P("pipe", "tensor", None)),
        check_vma=False,
    )
```

profile of v0, /device:TPU:26, one launch (start us, length us, event | category | flops | bytes accessed | tf_op | source)
XLA Modules:
  0.0 470.4 jit_solution(17740369245081746752)
XLA Ops:
  10.8 3.5 collective-permute-done
  14.9 24.3 %all-reduce.8 = bf16[128,512]{1,0:T(8,128)(2,1)S(1)} all-reduce(f32[128,512]{1,0:T(8,128)S(1)} %fusion.15), channel_id=1, replica_groups=mesh['pipe'=4,'seq'=16,'tensor'=8] {'tensor'}, use_global_device_ids=true, to_apply=%region_1.0 | all-reduce | flops 65536 | bytes 393216 | tf_op jit(solution)/shard_map/psum | solution.py:55
  41.0 149.0 %all-reduce.5.cloned.1.call-done = f32[1024,512]{0,1:T(8,128)} async-done(((f32[1024,512]{0,1:T(8,128)}), f32[1024,512]{0,1:T(8,128)}) %all-reduce.5.cloned.1.call-update) | async-done | bytes 2097168 | tf_op jit(solution)/shard_map/psum | solution.py:59
  190.0 6.7 %fusion.56 = f32[512,512]{0,1:T(8,128)} fusion(f32[1024,512]{0,1:T(8,128)} %all-reduce.5.cloned.1.call-done), kind=kOutput, calls=%fused_computation.103 | convolution fusion | flops 3221225472 | bytes 3145728 | tf_op jit(solution)/shard_map/dot_general | solution.py:60
  197.7 70.8 %all-reduce.7.cloned.1.call-done = f32[512,512]{0,1:T(8,128)} async-done(((f32[512,512]{0,1:T(8,128)}), f32[512,512]{0,1:T(8,128)}) %all-reduce.7.cloned.1.call-update) | async-done | bytes 1048592 | tf_op jit(solution)/shard_map/psum | solution.py:61
  271.4 11.7 %cholesky.104 = f32[128,128]{1,0:T(8,128)S(1)} custom-call(f32[128,128]{1,0:T(8,128)S(1)} %cholesky.266), custom_call_target="Cholesky" | custom-call | tf_op jit(solution)/shard_map/jit(cholesky)/cholesky | solution.py:23
  283.3 9.8 %custom-call.30 = f32[1,128,128]{1,2,0:T(8,128)S(1)} custom-call(f32[1,128,128]{2,1,0:T(8,128)S(1)} %get-tuple-element.31), custom_call_target="InvertDiagBlocksLowerTriangular" | custom-call | tf_op jit(solution)/shard_map/jit(cholesky)/cholesky | solution.py:23
  295.6 11.7 %cholesky.217 = f32[128,128]{1,0:T(8,128)S(1)} custom-call(f32[128,128]{1,0:T(8,128)S(1)} %cholesky.270), custom_call_target="Cholesky" | custom-call | tf_op jit(solution)/shard_map/jit(cholesky)/cholesky | solution.py:23
  307.4 10.0 %custom-call.31 = f32[1,128,128]{1,2,0:T(8,128)S(1)} custom-call(f32[1,128,128]{2,1,0:T(8,128)S(1)} %get-tuple-element.28), custom_call_target="InvertDiagBlocksLowerTriangular" | custom-call | tf_op jit(solution)/shard_map/jit(cholesky)/cholesky | solution.py:23
  319.1 11.7 %cholesky.238 = f32[128,128]{1,0:T(8,128)S(1)} custom-call(f32[128,128]{1,0:T(8,128)S(1)} %cholesky.275), custom_call_target="Cholesky" | custom-call | tf_op jit(solution)/shard_map/jit(cholesky)/cholesky | solution.py:23
  330.8 21.4 %all-gather.2.cloned.1.call-done = bf16[2048,1024]{1,0:T(8,128)(2,1)} async-done(((bf16[128,1024]{1,0:T(8,128)(2,1)}), bf16[2048,1024]{1,0:T(8,128)(2,1)}) %all-gather.2.cloned.1.call-update) | async-done | bytes 4194320 | tf_op jit(solution)/shard_map/all_gather | solution.py:45
  352.3 5.9 %convolution_convert_fusion = bf16[2048,512]{1,0:T(8,128)(2,1)} fusion(bf16[2048,1024]{1,0:T(8,128)(2,1)} %all-gather.2.cloned.1.call-done, bf16[1,512,1024]{2,1,0:T(8,128)(2,1)S(1)} %copy-done), kind=kOutput, calls=%fused_computation.2 | convolution fusion | flops 2148532224 | bytes 7340032 | tf_op jit(solution)/shard_map/dot_general | solution.py:44
  358.9 9.8 %custom-call.32 = f32[1,128,128]{1,2,0:T(8,128)S(1)} custom-call(f32[1,128,128]{2,1,0:T(8,128)S(1)} %get-tuple-element.25), custom_call_target="InvertDiagBlocksLowerTriangular" | custom-call | tf_op jit(solution)/shard_map/jit(cholesky)/cholesky | solution.py:23
  370.9 11.9 %cholesky.255 = f32[128,128]{1,0:T(8,128)S(1)} custom-call(f32[128,128]{1,0:T(8,128)S(1)} %convolution_subtract_fusion.4), custom_call_target="Cholesky" | custom-call | tf_op jit(solution)/shard_map/jit(cholesky)/cholesky | solution.py:23
  388.0 2.3 select_select_fusion
  390.4 13.6 %while.1 = (s32[]{:T(128)}, f32[512,512]{1,0:T(8,128)}, s32[4,2]{0,1:T(2,128)S(1)}, f32[4,128,128]{2,1,0:T(8,128)}, s32[]{:T(128)}) while((s32[]{:T(128)}, f32[512,512]{1,0:T(8,128)}, s32[4,2]{0,1:T(2,128)S(1)}, f32[4,128,128]{2,1,0:T(8,128)}, s32[]{:T(128)}) %tuple.35), condition=%wide.while_cond, body=%wide.while_body.sunk | while | flops 2 | bytes 132205 | solution.py:24
  391.0 2.8 bitcast_dynamic-update-slice_fusion.2
  394.4 2.8 bitcast_dynamic-update-slice_fusion.2
  397.8 2.8 bitcast_dynamic-update-slice_fusion.2
  401.2 2.8 bitcast_dynamic-update-slice_fusion.2
  404.0 40.1 %custom-call.33 = f32[4,128,128]{1,2,0:T(8,128)S(1)} custom-call(f32[4,128,128]{2,1,0:T(8,128)} %get-tuple-element.9), custom_call_target="InvertDiagBlocksLowerTriangular" | custom-call | tf_op jit(solution)/shard_map/triangular_solve | solution.py:24
  450.2 2.8 fusion.7
  453.0 2.4 collective-permute-start.1
  460.1 2.6 collective-permute-done.1
  (77 shorter events, 33.3 us)
Async XLA Ops:
  7.2 345.1 %copy-start = (bf16[1,512,1024]{2,1,0:T(8,128)(2,1)S(1)}, bf16[1,512,1024]{2,1,0:T(8,128)(2,1)}, u32[]{:S(2)}) copy-start(bf16[1,512,1024]{2,1,0:T(8,128)(2,1)} %param.10) | copy-start | bytes 3145732
  7.2 7.4 %copy-start.9 = (bf16[1,1024,512]{2,1,0:T(8,128)(2,1)S(1)}, bf16[1,1024,512]{2,1,0:T(8,128)(2,1)}, u32[]{:S(2)}) copy-start(bf16[1,1024,512]{2,1,0:T(8,128)(2,1)} %param.11) | copy-start | bytes 3145732
  7.2 32.0 %copy-start.10 = (bf16[1,128,1024]{2,1,0:T(8,128)(2,1)S(1)}, bf16[1,128,1024]{2,1,0:T(8,128)(2,1)}, u32[]{:S(2)}) copy-start(bf16[1,128,1024]{2,1,0:T(8,128)(2,1)} %param.6) | copy-start | bytes 786436
  7.2 182.8 %all-reduce.5.cloned.1.call-start = ((), (), s32[]{:S(2)}) async-start(), calls=%async_computation.3 | async-start | bytes 4194304 | tf_op jit(solution)/shard_map/psum | solution.py:59
  8.7 5.6 %collective-permute-start = (f32[3,1024]{1,0:T(4,128)S(1)}, f32[3,1024]{1,0:T(4,128)S(1)}, u32[]{:S(2)}, u32[]{:S(2)}) collective-permute-start(f32[3,1024]{1,0:T(4,128)S(1)} %slice.150), channel_id=1, source_target_pairs={{8,0},{16,8},{24,16},{32,24},{40,32},{48,40},{56,48},{64,56},{72,6... | collective-permute-start | bytes 36872 | tf_op jit(solution)/shard_map/ppermute | solution.py:14
  14.5 26.4 %copy-start.8 = (bf16[128,1024]{1,0:T(8,128)(2,1)}, bf16[128,1024]{1,0:T(8,128)(2,1)S(1)}, u32[]{:S(2)}) copy-start(bf16[128,1024]{1,0:T(8,128)(2,1)S(1)} %fusion.22) | copy-start | bytes 786436
  41.0 227.5 %all-reduce.7.cloned.1.call-start = ((), (), s32[]{:S(2)}) async-start(), calls=%async_computation.4 | async-start | bytes 2097152 | tf_op jit(solution)/shard_map/psum | solution.py:61
  196.7 155.5 %all-gather.2.cloned.1.call-start = ((), (), s32[]{:S(2)}) async-start(), calls=%async_computation.1 | async-start | bytes 4456448 | tf_op jit(solution)/shard_map/all_gather | solution.py:45
  197.5 255.5 %reduce-scatter.2.cloned.1.call-start = ((), (), s32[]{:S(2)}) async-start(), calls=%async_computation.2 | async-start | bytes 2359296 | tf_op jit(solution)/shard_map/reduce_scatter | solution.py:50
  268.5 1.7 copy-start.6
  270.4 1.0 copy-start.7
  317.6 40.5 %copy-start.4 = (f32[512,512]{1,0:T(8,128)}, f32[512,512]{1,0:T(8,128)S(1)}, u32[]{:S(2)}) copy-start(f32[512,512]{1,0:T(8,128)S(1)} %convolution_dynamic-update-slice_fusion) | copy-start | bytes 3145732
  358.2 85.9 %copy-start.1 = (f32[1024,512]{0,1:T(8,128)S(1)}, f32[1024,512]{0,1:T(8,128)}, u32[]{:S(2)}) copy-start(f32[1024,512]{0,1:T(8,128)} %all-reduce.5.cloned.1.call-done) | copy-start | bytes 6291460
  444.8 4.6 copy-start.2
  446.9 2.4 copy-start.3
  449.4 0.8 copy-start.5
  453.0 9.7 %collective-permute-start.1 = (bf16[256,512]{1,0:T(8,128)(2,1)}, bf16[256,512]{1,0:T(8,128)(2,1)S(1)}, u32[]{:S(2)}, u32[]{:S(2)}) collective-permute-start(bf16[256,512]{1,0:T(8,128)(2,1)} %reduce-scatter.2.cloned.1.call-done), channel_id=1, source_target_pairs={{0,384},{128,0},{256,128},{384,256},{1,385},{129,1},{257,129},{385... | collective-permute-start | bytes 786440 | tf_op jit(solution)/shard_map/ppermute | solution.py:19
Sparse Core Ops, SparseCore 0:
  41.1 148.8 all-reduce.4
  196.9 71.6 all-reduce.6
  271.2 81.0 all-gather.1
  358.3 33.8 reduce-scatter.1
where the time goes:
time: 475 us; the launch traced here: 470 us
  waiting for transfers between devices  248 us (52%)
  other arithmetic  127 us (27%)
  matrix products  30.8 us (6%)
  blocking collectives  24.3 us (5%)
  local copies, waits for them, and re-layouts  19.3 us (4%)
  between operations  17.2 us (4%)
    psum x1, waiting for transfers between devices, local(): sketch = lax.psum(sketch_part, 'seq')  149 us
    another operation x14, other arithmetic, finish_basis(): low = jnp.linalg.cholesky(gram)  79.9 us
    psum x1, waiting for transfers between devices, local(): gram = lax.psum(gram_part, 'tensor')  70.8 us
    another operation x3, other arithmetic, finish_basis(): lax.linalg.triangular_solve(low, sketch.T, left_side=True, lower=True)  42.5 us
    psum x1, blocking collectives, local(): sketch_rows = lax.psum(row_terms, 'tensor').astype(jnp.bfloat16)  24.3 us
    all_gather x1, waiting for transfers between devices, local(): lax.all_gather(in_grad, 'seq', axis=0, tiled=True)  21.4 us
    another operation x12, local copies, waits for them, and re-layouts  13.6 us
    another operation x7, matrix products, finish_basis(): lax.linalg.triangular_solve(low, sketch.T, left_side=True, lower=True)  9.66 us
  transfers between devices with their start and end apart: 6, of which 5 were waited for; matrix products, arithmetic and copies ran while one was open for 34% of the time, Pallas kernels for 0%

commit v1 on v0

v1 whole, which is shorter than its diff:
```python
import functools
import math

import jax
import jax.numpy as jnp
from jax import lax
from jax.experimental import pallas as pl
from jax.experimental.pallas import tpu as pltpu
from jax.sharding import PartitionSpec as P

D = 8192
F = jnp.float32
B = jnp.bfloat16
HI = lax.Precision.HIGHEST
VMEM = pl.BlockSpec(memory_space=pltpu.VMEM)
LIMIT = 32 * 1024 * 1024
WIDE = 58 * 1024 * 1024


def row_of(x, i):
    return jnp.broadcast_to(x[i:i+1, :], x.shape)
def lane_of(x, l):
    return jnp.broadcast_to(x[:, l:l+1], (x.shape[0], 128))

def leaf(work):
    sub = lax.broadcasted_iota(jnp.int32, (8, 128), 0)
    for p in range(16):
        pa = work[8*p:8*p+8, 0:128]
        pi = work[8*p:8*p+8, 128:256]
        cols = [lane_of(pa, 8*p+j) for j in range(8)]
        e = {}
        for j in range(8):
            for i in range(j, 8):
                e[i, j] = row_of(cols[j], i)
        x = {}; l = {}
        for j in range(8):
            r = lax.rsqrt(e[j, j])
            x[j, j] = r
            for i in range(j+1, 8):
                l[i, j] = e[i, j] * r
            for i in range(j+1, 8):
                for k in range(j+1, i+1):
                    e[i, k] = e[i, k] - l[i, j] * l[k, j]
        for j in range(8):
            for i in range(j+1, 8):
                acc = l[i, j] * x[j, j]
                for k in range(j+1, i):
                    acc = acc + l[i, k] * x[k, j]
                x[i, j] = -x[i, i] * acc
        ra = [row_of(pa, j) for j in range(8)]
        ri = [row_of(pi, j) for j in range(8)]
        ta = []; ti = []
        for i in range(8):
            a = x[i, 0]*ra[0]; b = x[i, 0]*ri[0]
            for j in range(1, i+1):
                a = a + x[i, j]*ra[j]; b = b + x[i, j]*ri[j]
            ta.append(a); ti.append(b)
        if p < 15:
            wa = []; wi = []
            for i in range(8):
                a = x[i, i]*ta[i]; b = x[i, i]*ti[i]
                for j in range(i+1, 8):
                    a = a + x[j, i]*ta[j]; b = b + x[j, i]*ti[j]
                wa.append(a); wi.append(b)
            for q in range(p+1, 16):
                qa = work[8*q:8*q+8, 0:128]
                qi = work[8*q:8*q+8, 128:256]
                cs = [lane_of(qa, 8*p+j) for j in range(8)]
                da = cs[0]*wa[0]; di = cs[0]*wi[0]
                for j in range(1, 8):
                    da = da + cs[j]*wa[j]; di = di + cs[j]*wi[j]
                work[8*q:8*q+8, 0:128] = qa - da
                work[8*q:8*q+8, 128:256] = qi - di
        ui = ti[0]
        for j in range(1, 8):
            ui = jnp.where(sub == j, ti[j], ui)
        work[8*p:8*p+8, 128:256] = ui

def dot(a, b, ca, cb, prec=HI):
    return lax.dot_general(a, b, (((ca,), (cb,)), ((), ())), precision=prec, preferred_element_type=F)

def split(x):
    hi = x.astype(B)
    return hi, (x - hi.astype(F)).astype(B)

def chol_kernel(scale, gram_ref, sketch_ref, out_ref, m, work):
    n = 4
    blk = 0
    for r in range(n):
        for c in range(r, n):
            m[r*128:(r+1)*128, c*128:(c+1)*128] = gram_ref[blk*128:(blk+1)*128, :]
            blk += 1
    eye = (lax.broadcasted_iota(jnp.int32, (128, 128), 0) == lax.broadcasted_iota(jnp.int32, (128, 128), 1)).astype(F)
    def stage(k, carry):
        base = pl.multiple_of(k*128, 128)
        work[:, 0:128] = m[pl.ds(base, 128), pl.ds(base, 128)]
        work[:, 128:256] = eye
        leaf(work)
        inv = work[:, 128:256]
        m[pl.ds(base, 128), pl.ds(base, 128)] = eye
        row = dot(inv, m[pl.ds(base, 128), :], 1, 0)
        m[pl.ds(base, 128), :] = row
        def update(j, carry):
            jb = pl.multiple_of(j*128, 128)
            ukj = m[pl.ds(base, 128), pl.ds(jb, 128)]
            m[pl.ds(jb, 128), pl.ds(base, 128)] = jnp.zeros((128, 128), F)
            m[pl.ds(jb, 128), :] -= dot(ukj, m[pl.ds(base, 128), :], 0, 0)
            return carry
        lax.fori_loop(k+1, n, update, 0)
        return carry
    lax.fori_loop(0, n, stage, 0)
    for r in range(n):
        for c in range(r+1, n):
            m[r*128:(r+1)*128, c*128:(c+1)*128] = jnp.zeros((128, 128), F)
    th, tl = split(m[...] * scale)
    def body(i, carry):
        b = pl.multiple_of(i*256, 256)
        sh, sl = split(sketch_ref[pl.ds(b, 256), :])
        d = dot(sh, th, 1, 1, None) + (dot(sh, tl, 1, 1, None) + dot(sl, th, 1, 1, None))
        out_ref[pl.ds(b, 256), :] = d.astype(B)
        return carry
    lax.fori_loop(0, sketch_ref.shape[0]//256, body, 0)

def finish(gram_packed, sketch, scale, **kw):
    return pl.pallas_call(
        functools.partial(chol_kernel, scale),
        out_shape=jax.ShapeDtypeStruct(sketch.shape, B),
        in_specs=[pl.BlockSpec(memory_space=pltpu.VMEM)]*2,
        out_specs=pl.BlockSpec(memory_space=pltpu.VMEM),
        scratch_shapes=[pltpu.VMEM((512, 512), F), pltpu.VMEM((128, 256), F)],
        compiler_params=pltpu.CompilerParams(vmem_limit_bytes=LIMIT), **kw,
    )(gram_packed, sketch)


def front_kernel(conv_ref, act_ref, next_ref, taps_ref, acts_ref, test_ref, both_ref, rows_ref, held):
    rows = conv_ref.shape[0]

    def pre(p, g):
        sig = jax.nn.sigmoid(p)
        return g * sig * (1.0 + p * (1.0 - sig))

    held[0:rows, :] = pre(conv_ref[...].astype(F), act_ref[...].astype(F))
    after = next_ref[...].astype(F)
    held[rows : rows + 8, :] = pre(after[0:8, :], after[8:16, :])
    taps = taps_ref[...].astype(F)
    total = taps[0:1, :] * held[0:rows, :]
    for tap in range(1, taps.shape[0]):
        total = total + taps[tap : tap + 1, :] * held[tap : tap + rows, :]
    grad = total.astype(B)
    both_ref[0:rows, :] = acts_ref[...]
    both_ref[rows : 2 * rows, :] = grad
    rows_ref[...] = jnp.dot(grad, test_ref[...], preferred_element_type=F)


def front(conv, act, after, taps, acts, test):
    rows, width = conv.shape
    return pl.pallas_call(
        front_kernel,
        out_shape=(
            jax.ShapeDtypeStruct((2 * rows, width), B),
            jax.ShapeDtypeStruct((rows, test.shape[1]), F),
        ),
        scratch_shapes=[pltpu.VMEM((rows + 8, width), F)],
        compiler_params=pltpu.CompilerParams(vmem_limit_bytes=WIDE),
    )(conv, act, after, taps, acts, test)


def grad_kernel(grad_ref, weight_ref, out_ref):
    grad = grad_ref[...].reshape(-1, grad_ref.shape[-1])
    out_ref[...] = lax.dot_general(
        grad, weight_ref[...], (((1,), (1,)), ((), ())), preferred_element_type=F
    ).astype(B)


def grad_terms(gathered, weights):
    shards, twice, width = gathered.shape
    rows = twice // 2
    each = 4
    return pl.pallas_call(
        grad_kernel,
        grid=(shards // each,),
        out_shape=jax.ShapeDtypeStruct((shards * rows, weights.shape[0]), B),
        in_specs=[
            pl.BlockSpec((each, rows, width), lambda i: (i, 1, 0)),
            pl.BlockSpec(weights.shape, lambda i: (0, 0)),
        ],
        out_specs=pl.BlockSpec((each * rows, weights.shape[0]), lambda i: (i, 0)),
        compiler_params=pltpu.CompilerParams(vmem_limit_bytes=WIDE),
    )(gathered, weights)


def sketch_kernel(acts_ref, rows_ref, sketch_ref, gram_ref):
    groups, shards, share, rank = rows_ref.shape
    cols = acts_ref.shape[-1]
    part = jnp.zeros((cols, rank), F)
    for g in range(groups):
        acts = acts_ref[:, g * share : (g + 1) * share, :].reshape(shards * share, cols)
        rows = rows_ref[g].reshape(shards * share, rank)
        part += lax.dot_general(acts, rows, (((0,), (0,)), ((), ())), preferred_element_type=F)
    sketch_ref[...] = part

    @pl.when(pl.program_id(0) == 0)
    def _():
        gram_ref[...] = jnp.zeros(gram_ref.shape, F)

    at = 0
    for r in range(part.shape[1] // 128):
        terms = dot(part[:, r * 128 : (r + 1) * 128], part[:, r * 128 :], 0, 0)
        for c in range(terms.shape[1] // 128):
            gram_ref[at : at + 128, :] += terms[:, c * 128 : (c + 1) * 128]
            at += 128


def sketch_and_gram(gathered, rows):
    shards, twice, width = gathered.shape
    cols = 256
    rank = rows.shape[-1]
    blocks = rank // 128
    packed = blocks * (blocks + 1) // 2 * 128
    return pl.pallas_call(
        sketch_kernel,
        grid=(width // cols,),
        out_shape=(
            jax.ShapeDtypeStruct((width, rank), F),
            jax.ShapeDtypeStruct((packed, 128), F),
        ),
        in_specs=[
            pl.BlockSpec((shards, twice // 2, cols), lambda i: (0, 0, i)),
            pl.BlockSpec(rows.shape, lambda i: (0, 0, 0, 0)),
        ],
        out_specs=(
            pl.BlockSpec((cols, rank), lambda i: (i, 0)),
            pl.BlockSpec((packed, 128), lambda i: (0, 0)),
        ),
        compiler_params=pltpu.CompilerParams(vmem_limit_bytes=WIDE),
    )(gathered, rows)


def gathered_rows(terms):
    groups = lax.axis_size("tensor")
    rank = terms.shape[1]
    terms = lax.all_to_all(terms.reshape(groups, -1, rank), "tensor", 0, 0, tiled=True)
    rows = jnp.sum(terms, axis=0).astype(B)
    rows = lax.all_gather(rows, "seq", axis=0)
    return lax.all_to_all(
        jnp.broadcast_to(rows[None], (groups,) + rows.shape), "tensor", 0, 0, tiled=True
    )


def local(layer_input, conv_out, act_grad, conv_kernel, in_proj, sketch_matrix):
    conv, act = conv_out[0], act_grad[0]
    shards = lax.axis_size("seq")
    after = lax.ppermute(
        jnp.concatenate([conv[:8], act[:8]], axis=0),
        "seq",
        [(i + 1, i) for i in range(shards - 1)],
    )
    both, row_terms = front(conv, act, after, conv_kernel[0], layer_input[0], sketch_matrix[0])
    gathered = lax.all_gather(both, "seq", axis=0)
    rows = gathered_rows(row_terms)
    gathered, rows = lax.optimization_barrier((gathered, rows))
    terms = grad_terms(gathered, in_proj[0])
    input_grad = lax.psum_scatter(terms, "tensor", scatter_dimension=0, tiled=True)
    count = lax.axis_size("pipe")
    passed = lax.ppermute(input_grad, "pipe", [(i, (i - 1) % count) for i in range(count)])
    sketch, gram = sketch_and_gram(gathered, rows)
    groups = lax.axis_size("tensor")
    gram = lax.all_to_all(gram.reshape(groups, -1, 128), "tensor", 0, 0, tiled=True)
    gram = lax.all_gather(jnp.sum(gram, axis=0), "tensor", axis=0, tiled=True)
    basis = finish(gram, sketch, math.sqrt(D))
    return (passed[None], basis[None])


def solution(mesh):
    placed = (
        P("pipe", "seq", "tensor"),
        P("pipe", "seq", "tensor"),
        P("pipe", "seq", "tensor"),
        P("pipe", None, "tensor"),
        P("pipe", "seq", "tensor"),
        P("pipe", "tensor", None),
    )
    return jax.shard_map(
        local,
        mesh=mesh,
        in_specs=placed,
        out_specs=(P("pipe", "tensor", "seq"), P("pipe", "tensor", None)),
        check_vma=False,
    )
```

time: 475 us -> 233 us (0.49)
  the two profiles are of different devices: /device:TPU:26 before, /device:TPU:1 now
where the time goes in v1:
time: 233 us
  blocking collectives  116 us (50%)
  waiting for transfers between devices  49.5 us (21%)
  Pallas kernels  46.1 us (20%)
  between operations  14.1 us (6%)
  starting transfers between devices  5.07 us (2%)
    all_to_all x1, blocking collectives, gathered_rows(): lax.all_to_all(jnp.broadcast_to(rows[None], (groups,) + rows.shape), 'ten...  35.3 us
    all_gather x1, waiting for transfers between devices, local(): gathered = lax.all_gather(both, 'seq', axis=0)  31.3 us
    all_gather x1, blocking collectives, gathered_rows(): rows = lax.all_gather(rows, 'seq', axis=0)  30 us
    pallas_call x1, Pallas kernels, finish(): pl.pallas_call(functools.partial(chol_kernel, scale), out_shape=jax.Shape...  27.8 us
    all_to_all x1, blocking collectives, local(): lax.all_to_all(gram.reshape(groups, -1, 128), 'tensor', 0, 0, tiled=True)  18.8 us
    all_to_all x1, blocking collectives, gathered_rows(): lax.all_to_all(terms.reshape(groups, -1, rank), 'tensor', 0, 0, tiled=True)  16.8 us
    all_gather x1, blocking collectives, local(): gram = lax.all_gather(jnp.sum(gram, axis=0), 'tensor', axis=0, tiled=True)  14.6 us
    reduce_scatter x1, waiting for transfers between devices, local(): lax.psum_scatter(terms, 'tensor', scatter_dimension=0, tiled=True)  13.8 us
  transfers between devices with their start and end apart: 4, of which 3 were waited for; matrix products, arithmetic and copies ran while one was open for 0% of the time, Pallas kernels for 16%

profile of v1, /device:TPU:1, one launch (start us, length us, event | category | flops | bytes accessed | tf_op | source)
XLA Modules:
  0.0 232.8 jit_solution(8491322396972815803)
XLA Ops:
  7.2 0.0 all-gather.4.cloned.1.call-start
  7.2 0.7 slice_bitcast_fusion
  8.0 1.3 collective-permute-start
  9.2 4.4 %collective-permute-done.next_ref = bf16[16,1024]{1,0:T(8,128)(2,1)S(1)} collective-permute-done((bf16[16,1024]{1,0:T(8,128)(2,1)S(1)}, bf16[16,1024]{1,0:T(8,128)(2,1)S(1)}, u32[]{:S(2)}, u32[]{:S(2)}) %collective-permute-start) | collective-permute-done | bytes 32800 | tf_op jit(solution)/shard_map/ppermute | solution.py:253
  13.6 0.6 copy-done.1
  14.2 2.9 %shard_map.77 = (bf16[256,1024]{1,0:T(8,128)(2,1)}, f32[128,512]{1,0:T(8,128)}) custom-call(bf16[128,1024]{1,0:T(8,128)(2,1)} %bitcast.23, bf16[128,1024]{1,0:T(8,128)(2,1)} %bitcast.24, bf16[16,1024]{1,0:T(8,128)(2,1)} %copy-done.1, bf16[4,1024]{1,0:T(4,128)(2,1)} %bitcast.28, bf16[128,1024]{1,0:T(8,128)(2,1)} %bitcast.25, bf16[1024,512]{1,0:T(8,128)(2,1)} %bitcast.18), custom_call_target="tpu_custom_call" | custom-call | tf_op jit(solution)/shard_map/pallas_call | solution.py:157
  17.1 0.0 all-gather.4.cloned.1.call-update
  17.2 0.0 reduce-scatter.2.cloned.1.call-start
  17.2 16.8 %all_to_all.15 = f32[8,16,512]{2,1,0:T(8,128)S(1)} all-to-all(f32[8,16,512]{2,1,0:T(8,128)} %bitcast.26), channel_id=1, replica_groups=mesh['pipe'=4,'seq'=16,'tensor'=8] {'tensor'}, dimensions={0} | all-to-all | bytes 524288 | tf_op jit(solution)/shard_map/all_to_all | solution.py:242
  34.1 30.0 %all-gather.1 = bf16[256,512]{1,0:T(8,128)(2,1)S(1)} all-gather(bf16[16,512]{1,0:T(8,128)(2,1)S(1)} %reduce_sum.18), channel_id=3, replica_groups=mesh['pipe'=4,'seq'=16,'tensor'=8] {'seq'}, dimensions={0}, use_global_device_ids=true | all-gather | bytes 278528 | tf_op jit(solution)/shard_map/all_gather | solution.py:244
  64.0 0.3 broadcast_in_dim.12
  64.3 35.3 %all_to_all.16.rows_ref = bf16[8,16,16,512]{3,2,1,0:T(8,128)(2,1)} all-to-all(bf16[8,16,16,512]{3,2,1,0:T(8,128)(2,1)S(1)} %broadcast_in_dim.12), channel_id=1, replica_groups=mesh['pipe'=4,'seq'=16,'tensor'=8] {'tensor'}, dimensions={0} | all-to-all | bytes 4194304 | tf_op jit(solution)/shard_map/all_to_all | solution.py:245
  99.6 31.3 %all-gather.4.cloned.1.call-done = bf16[4096,1024]{1,0:T(8,128)(2,1)} async-done(((bf16[256,1024]{1,0:T(8,128)(2,1)}), bf16[4096,1024]{1,0:T(8,128)(2,1)}) %all-gather.4.cloned.1.call-update) | async-done | bytes 8388624 | tf_op jit(solution)/shard_map/all_gather | solution.py:259
  131.0 6.1 %shard_map.78 = bf16[2048,512]{1,0:T(8,128)(2,1)} custom-call(bf16[16,256,1024]{2,1,0:T(8,128)(2,1)} %bitcast.16, bf16[512,1024]{1,0:T(8,128)(2,1)} %bitcast.21), custom_call_target="tpu_custom_call" | custom-call | tf_op jit(solution)/shard_map/pallas_call | solution.py:179
  137.1 0.0 reduce-scatter.2.cloned.1.call-update
  137.1 9.3 %shard_map.79 = (f32[1024,512]{1,0:T(8,128)}, f32[1280,128]{1,0:T(8,128)}) custom-call(bf16[16,256,1024]{2,1,0:T(8,128)(2,1)} %bitcast.17, bf16[8,16,16,512]{3,2,1,0:T(8,128)(2,1)} %all_to_all.16.rows_ref), custom_call_target="tpu_custom_call" | custom-call | tf_op jit(solution)/shard_map/pallas_call | solution.py:220
  146.4 18.8 %all_to_all.17 = f32[8,160,128]{2,1,0:T(8,128)S(1)} all-to-all(f32[8,160,128]{2,1,0:T(8,128)} %bitcast.22), channel_id=1, replica_groups=mesh['pipe'=4,'seq'=16,'tensor'=8] {'tensor'}, dimensions={0} | all-to-all | bytes 1310720 | tf_op jit(solution)/shard_map/all_to_all | solution.py:268
  165.3 13.8 %reduce-scatter.2.cloned.1.call-done = bf16[256,512]{1,0:T(8,128)(2,1)} async-done(((bf16[2048,512]{1,0:T(8,128)(2,1)}), bf16[256,512]{1,0:T(8,128)(2,1)}) %reduce-scatter.2.cloned.1.call-update) | async-done | bytes 262160 | tf_op jit(solution)/shard_map/reduce_scatter | solution.py:263
  179.1 3.7 %collective-permute-start.1 = (bf16[256,512]{1,0:T(8,128)(2,1)}, bf16[256,512]{1,0:T(8,128)(2,1)S(1)}, u32[]{:S(2)}, u32[]{:S(2)}) collective-permute-start(bf16[256,512]{1,0:T(8,128)(2,1)} %reduce-scatter.2.cloned.1.call-done), channel_id=1, source_target_pairs={{0,384},{128,0},{256,128},{384,256},{1,385},{129,1},{257,129},{385... | collective-permute-start | bytes 786440 | tf_op jit(solution)/shard_map/ppermute | solution.py:265
  182.8 14.6 %all_gather.16.gram_ref = f32[1280,128]{1,0:T(8,128)S(1)} all-gather(f32[160,128]{1,0:T(8,128)S(1)} %reduce_sum.19), channel_id=1, replica_groups=mesh['pipe'=4,'seq'=16,'tensor'=8] {'tensor'}, dimensions={0}, use_global_device_ids=true | all-gather | bytes 737280 | tf_op jit(solution)/shard_map/all_gather | solution.py:269
  197.4 0.0 copy-done
  197.4 27.8 %shard_map.80 = bf16[1024,512]{1,0:T(8,128)(2,1)} custom-call(f32[1280,128]{1,0:T(8,128)S(1)} %all_gather.16.gram_ref, f32[1024,512]{1,0:T(8,128)S(1)} %copy-done), custom_call_target="tpu_custom_call" | custom-call | tf_op jit(solution)/shard_map/pallas_call | solution.py:125
  225.2 0.0 collective-permute-done.1
  225.2 0.7 copy.9
  (5 shorter events, 0.1 us)
Async XLA Ops:
  7.2 123.8 %all-gather.4.cloned.1.call-start = ((), (), s32[]{:S(2)}) async-start(), calls=%async_computation.5 | async-start | bytes 8912896 | tf_op jit(solution)/shard_map/all_gather | solution.py:259
  8.0 5.7 %collective-permute-start = (bf16[16,1024]{1,0:T(8,128)(2,1)S(1)}, bf16[16,1024]{1,0:T(8,128)(2,1)S(1)}, u32[]{:S(2)}, u32[]{:S(2)}) collective-permute-start(bf16[16,1024]{1,0:T(8,128)(2,1)S(1)} %pad_maximum_fusion), channel_id=1, source_target_pairs={{8,0},{16,8},{24,16},{32,24},{40,32},{48,40},{56,48},{64,56},{72,6... | collective-permute-start | bytes 98312 | tf_op jit(solution)/shard_map/ppermute | solution.py:253
  13.6 0.6 copy-start.1
  17.2 161.9 %reduce-scatter.2.cloned.1.call-start = ((), (), s32[]{:S(2)}) async-start(), calls=%async_computation.4 | async-start | bytes 2359296 | tf_op jit(solution)/shard_map/reduce_scatter | solution.py:263
  146.4 51.0 %copy-start = (f32[1024,512]{1,0:T(8,128)S(1)}, f32[1024,512]{1,0:T(8,128)}, u32[]{:S(2)}) copy-start(f32[1024,512]{1,0:T(8,128)} %get-tuple-element.13.sketch_ref) | copy-start | bytes 6291460
  179.1 46.2 %collective-permute-start.1 = (bf16[256,512]{1,0:T(8,128)(2,1)}, bf16[256,512]{1,0:T(8,128)(2,1)S(1)}, u32[]{:S(2)}, u32[]{:S(2)}) collective-permute-start(bf16[256,512]{1,0:T(8,128)(2,1)} %reduce-scatter.2.cloned.1.call-done), channel_id=1, source_target_pairs={{0,384},{128,0},{256,128},{384,256},{1,385},{129,1},{257,129},{385... | collective-permute-start | bytes 786440 | tf_op jit(solution)/shard_map/ppermute | solution.py:265
Sparse Core Ops, SparseCore 0:
  17.3 113.6 all-gather.3
  137.2 41.8 reduce-scatter.1

commit v2 on v0

v2 whole, which is shorter than its diff:
```python
import functools
import math

import jax
import jax.numpy as jnp
from jax import lax
from jax.experimental import pallas as pl
from jax.experimental.pallas import tpu as pltpu
from jax.sharding import PartitionSpec as P

D = 8192
F = jnp.float32
B = jnp.bfloat16
HI = lax.Precision.HIGHEST
VMEM = pl.BlockSpec(memory_space=pltpu.VMEM)
ANY = pl.BlockSpec(memory_space=pl.ANY)
LIMIT = 32 * 1024 * 1024
WIDE = 58 * 1024 * 1024
EDGE = 16


def dot(a, b, ca, cb, prec=HI):
    return lax.dot_general(
        a, b, (((ca,), (cb,)), ((), ())), precision=prec, preferred_element_type=F
    )


def split(x):
    hi = x.astype(B)
    return hi, (x - hi.astype(F)).astype(B)


def total_of(values):
    values = list(values)
    while len(values) > 1:
        values = [
            values[i] + values[i + 1] if i + 1 < len(values) else values[i]
            for i in range(0, len(values), 2)
        ]
    return values[0]


def pre_grad(p, g):
    sig = jax.nn.sigmoid(p)
    return g * sig * (1.0 + p * (1.0 - sig))


def convolved(held, taps, rows):
    total = taps[0:1, :] * held[0:rows, :]
    for tap in range(1, taps.shape[0]):
        total = total + taps[tap : tap + 1, :] * held[tap : tap + rows, :]
    return total.astype(B)


def front_kernel(conv_ref, act_ref, taps_ref, acts_ref, both_ref, held):
    rows = conv_ref.shape[0]
    held[0:rows, :] = pre_grad(conv_ref[...].astype(F), act_ref[...].astype(F))
    held[rows : rows + 8, :] = jnp.zeros((8, held.shape[1]), F)
    both_ref[0:rows, :] = acts_ref[...]
    both_ref[rows : 2 * rows, :] = convolved(held, taps_ref[...].astype(F), rows)


def front(conv, act, taps, acts):
    rows, width = conv.shape
    return pl.pallas_call(
        front_kernel,
        out_shape=jax.ShapeDtypeStruct((2 * rows, width), B),
        scratch_shapes=[pltpu.VMEM((rows + 8, width), F)],
        compiler_params=pltpu.CompilerParams(vmem_limit_bytes=WIDE),
    )(conv, act, taps, acts)


def edge_kernel(conv_ref, act_ref, next_ref, taps_ref, grad_ref, test_ref, rows_ref, edge_ref, held):
    held[0:EDGE, :] = pre_grad(conv_ref[...].astype(F), act_ref[...].astype(F))
    after = next_ref[...].astype(F)
    held[EDGE : EDGE + 8, :] = pre_grad(after[0:8, :], after[8:16, :])
    edge = convolved(held, taps_ref[...].astype(F), EDGE)
    half = edge.shape[1] // 2
    edge_ref[0:EDGE, :] = edge[:, 0:half]
    edge_ref[EDGE : 2 * EDGE, :] = edge[:, half:]
    rows = grad_ref.shape[0]
    grad = jnp.concatenate([grad_ref[0 : rows - EDGE, :], edge], axis=0)
    rows_ref[...] = jnp.dot(grad, test_ref[...], preferred_element_type=F)


def edge_and_rows(conv, act, after, taps, both, test):
    rows, width = conv.shape
    rank = test.shape[1]
    last = rows // EDGE - 1

    def whole(*shape):
        return pl.BlockSpec(shape, lambda i: (0, 0))

    return pl.pallas_call(
        edge_kernel,
        grid=(1,),
        out_shape=(
            jax.ShapeDtypeStruct((rows, rank), F),
            jax.ShapeDtypeStruct((2 * EDGE, width // 2), B),
        ),
        in_specs=[
            pl.BlockSpec((EDGE, width), lambda i: (last, 0)),
            pl.BlockSpec((EDGE, width), lambda i: (last, 0)),
            whole(*after.shape),
            whole(*taps.shape),
            pl.BlockSpec((rows, width), lambda i: (1, 0)),
            whole(*test.shape),
        ],
        out_specs=(whole(rows, rank), whole(2 * EDGE, width // 2)),
        scratch_shapes=[pltpu.VMEM((EDGE + 8, width), F)],
        compiler_params=pltpu.CompilerParams(vmem_limit_bytes=WIDE),
    )(conv, act, after, taps, both, test)


CHUNKS = 4


def middle_kernel(
    both_ref, rows_ref, edge_ref, weight_ref, sketch_ref, gram_ref, terms_ref,
    acts, grads, terms, right_all, weights, in_sems, out_sems,
):
    shards, twice, width = both_ref.shape
    tokens = twice // 2
    groups, _, share, rank = rows_ref.shape
    cols = width // CHUNKS
    each = shards // CHUNKS

    def acts_copy(i):
        return pltpu.make_async_copy(
            both_ref.at[:, 0:tokens, i * cols : (i + 1) * cols], acts.at[i], in_sems.at[i]
        )

    def grads_copy(i):
        return pltpu.make_async_copy(
            both_ref.at[i * each : (i + 1) * each, tokens:twice, :], grads.at[i], in_sems.at[CHUNKS + i]
        )

    def terms_copy(i):
        return pltpu.make_async_copy(
            terms.at[i], terms_ref.at[i * each * tokens : (i + 1) * each * tokens, :], out_sems.at[i]
        )

    rows_copy = pltpu.make_async_copy(rows_ref, right_all, in_sems.at[2 * CHUNKS])
    weight_copy = pltpu.make_async_copy(weight_ref, weights, in_sems.at[2 * CHUNKS + 1])
    acts_copy(0).start()
    rows_copy.start()
    for i in range(1, CHUNKS):
        acts_copy(i).start()
    weight_copy.start()
    for i in range(CHUNKS):
        grads_copy(i).start()
    rows_copy.wait()
    for i in range(CHUNKS):
        acts_copy(i).wait()
        part = jnp.zeros((cols, rank), F)
        for g in range(groups):
            left = acts[i, :, g * share : (g + 1) * share, :].reshape(shards * share, cols)
            right = right_all[g].reshape(shards * share, rank)
            part += dot(left, right, 0, 0, None)
        sketch_ref[i * cols : (i + 1) * cols, :] = part
        at = 0
        for r in range(rank // 128):
            block = dot(part[:, r * 128 : (r + 1) * 128], part[:, r * 128 :], 0, 0)
            for c in range(block.shape[1] // 128):
                piece = block[:, c * 128 : (c + 1) * 128]
                if i == 0:
                    gram_ref[at : at + 128, :] = piece
                else:
                    gram_ref[at : at + 128, :] += piece
                at += 128
    half = width // 2
    weight_copy.wait()
    for i in range(CHUNKS):
        grads_copy(i).wait()
        for z in range(each):
            edge = edge_ref[i * each + z]
            grads[i, z, tokens - EDGE : tokens, 0:half] = edge[0:EDGE, :]
            grads[i, z, tokens - EDGE : tokens, half:] = edge[EDGE : 2 * EDGE, :]
        left = grads[i].reshape(each * tokens, width)
        terms[i] = dot(left, weights[...], 1, 1, None).astype(B)
        terms_copy(i).start()
    for i in range(CHUNKS):
        terms_copy(i).wait()


def middle(gathered, rows, edges, weights):
    shards, twice, width = gathered.shape
    tokens = twice // 2
    rank = rows.shape[-1]
    blocks = rank // 128
    packed = blocks * (blocks + 1) // 2 * 128
    outs = weights.shape[0]
    each = shards // CHUNKS
    return pl.pallas_call(
        middle_kernel,
        out_shape=(
            jax.ShapeDtypeStruct((width, rank), F),
            jax.ShapeDtypeStruct((packed, 128), F),
            jax.ShapeDtypeStruct((shards * tokens, outs), B),
        ),
        in_specs=[ANY, ANY, VMEM, ANY],
        out_specs=(VMEM, VMEM, ANY),
        scratch_shapes=[
            pltpu.VMEM((CHUNKS, shards, tokens, width // CHUNKS), B),
            pltpu.VMEM((CHUNKS, each, tokens, width), B),
            pltpu.VMEM((CHUNKS, each * tokens, outs), B),
            pltpu.VMEM(rows.shape, B),
            pltpu.VMEM(weights.shape, B),
            pltpu.SemaphoreType.DMA((2 * CHUNKS + 2,)),
            pltpu.SemaphoreType.DMA((CHUNKS,)),
        ],
        compiler_params=pltpu.CompilerParams(vmem_limit_bytes=WIDE),
    )(gathered, rows, edges, weights)


def lane_of(x, l):
    return jnp.broadcast_to(x[:, l : l + 1], (8, 128))


def row_of(ref, r, c):
    return jnp.broadcast_to(ref[r : r + 1, c : c + 128], (8, 128))


def leaf(work, staged):
    sub = lax.broadcasted_iota(jnp.int32, (8, 128), 0)
    for p in range(16):
        top = 8 * p
        panel = work[top : top + 8, 0:128]
        left = [row_of(work, top + j, 0) for j in range(8)]
        right = [row_of(work, top + j, 128) for j in range(8)]
        e = {}
        for j in range(8):
            staged[8 * j : 8 * j + 8, :] = lane_of(panel, top + j)
            for i in range(j, 8):
                e[i, j] = row_of(staged, 8 * j + i, 0)
        inv = {}
        acc = {}
        for j in range(8):
            r = lax.rsqrt(e[j, j])
            low = {i: e[i, j] * r for i in range(j + 1, 8)}
            for i in range(j + 1, 8):
                for k in range(j + 1, i + 1):
                    e[i, k] = e[i, k] - low[i] * low[k]
            left[j] = left[j] * r
            right[j] = right[j] * r
            for k in range(j):
                inv[j, k] = -(acc[j, k] * r)
            inv[j, j] = r
            for i in range(j + 1, 8):
                left[i] = left[i] - low[i] * left[j]
                right[i] = right[i] - low[i] * right[j]
                for k in range(j + 1):
                    t = low[i] * inv[j, k]
                    acc[i, k] = acc[i, k] + t if (i, k) in acc else t
        rows = right[0]
        for j in range(1, 8):
            rows = jnp.where(sub == j, right[j], rows)
        work[top : top + 8, 128:256] = rows
        if p == 15:
            break
        whole_left = []
        whole_right = []
        for i in range(8):
            a = inv[i, i] * left[i]
            b = inv[i, i] * right[i]
            for j in range(i + 1, 8):
                a = a + inv[j, i] * left[j]
                b = b + inv[j, i] * right[j]
            whole_left.append(a)
            whole_right.append(b)
        for q in range(top + 8, 128, 8):
            old = work[q : q + 8, 0:128]
            by = [lane_of(old, top + j) for j in range(8)]
            work[q : q + 8, 0:128] = old - total_of(by[j] * whole_left[j] for j in range(8))
            work[q : q + 8, 128:256] -= total_of(by[j] * whole_right[j] for j in range(8))


def stage(k, blocks, m, work, staged):
    eye = (
        lax.broadcasted_iota(jnp.int32, (128, 128), 0)
        == lax.broadcasted_iota(jnp.int32, (128, 128), 1)
    ).astype(F)
    base = pl.multiple_of(k * 128, 128)
    work[:, 0:128] = m[pl.ds(base, 128), pl.ds(base, 128)]
    work[:, 128:256] = eye
    leaf(work, staged)
    m[pl.ds(base, 128), pl.ds(base, 128)] = eye
    m[pl.ds(base, 128), :] = dot(work[:, 128:256], m[pl.ds(base, 128), :], 1, 0)

    def update(j, carry):
        at = pl.multiple_of(j * 128, 128)
        factor = m[pl.ds(base, 128), pl.ds(at, 128)]
        m[pl.ds(at, 128), pl.ds(base, 128)] = jnp.zeros((128, 128), F)
        m[pl.ds(at, 128), :] -= dot(factor, m[pl.ds(base, 128), :], 0, 0)
        return carry

    lax.fori_loop(k + 1, blocks, update, 0)


def factor_kernel(blocks, stages, gram_ref, m, work, staged):
    at = 0
    for r in range(blocks):
        for c in range(blocks):
            if c < r:
                m[r * 128 : (r + 1) * 128, c * 128 : (c + 1) * 128] = jnp.zeros((128, 128), F)
            else:
                m[r * 128 : (r + 1) * 128, c * 128 : (c + 1) * 128] = gram_ref[at : at + 128, :]
                at += 128

    def body(k, carry):
        stage(k, blocks, m, work, staged)
        return carry

    lax.fori_loop(0, stages, body, 0)


def apply_kernel(blocks, stages, scale, part_ref, sketch_ref, out_ref, m, work, staged):
    m[...] = part_ref[...]

    def body(k, carry):
        stage(k, blocks, m, work, staged)
        return carry

    lax.fori_loop(stages, blocks, body, 0)
    for r in range(blocks):
        for c in range(r + 1, blocks):
            m[r * 128 : (r + 1) * 128, c * 128 : (c + 1) * 128] = jnp.zeros((128, 128), F)
    inv_hi, inv_lo = split(m[...] * scale)

    def rows(i, carry):
        at = pl.multiple_of(i * 256, 256)
        hi, lo = split(sketch_ref[pl.ds(at, 256), :])
        out = dot(hi, inv_hi, 1, 1, None) + (dot(hi, inv_lo, 1, 1, None) + dot(lo, inv_hi, 1, 1, None))
        out_ref[pl.ds(at, 256), :] = out.astype(B)
        return carry

    lax.fori_loop(0, sketch_ref.shape[0] // 256, rows, 0)


FIRST = 3


def factored(gram_packed, rank):
    blocks = rank // 128
    return pl.pallas_call(
        functools.partial(factor_kernel, blocks, FIRST),
        out_shape=jax.ShapeDtypeStruct((rank, rank), F),
        in_specs=[VMEM],
        out_specs=VMEM,
        scratch_shapes=[pltpu.VMEM((128, 256), F), pltpu.VMEM((64, 128), F)],
        compiler_params=pltpu.CompilerParams(vmem_limit_bytes=LIMIT),
    )(gram_packed)


def applied(part, sketch, scale):
    rank = sketch.shape[1]
    return pl.pallas_call(
        functools.partial(apply_kernel, rank // 128, FIRST, scale),
        out_shape=jax.ShapeDtypeStruct(sketch.shape, B),
        in_specs=[VMEM] * 2,
        out_specs=VMEM,
        scratch_shapes=[
            pltpu.VMEM((rank, rank), F),
            pltpu.VMEM((128, 256), F),
            pltpu.VMEM((64, 128), F),
        ],
        compiler_params=pltpu.CompilerParams(vmem_limit_bytes=LIMIT),
    )(part, sketch)


def local(layer_input, conv_out, act_grad, conv_kernel, in_proj, sketch_matrix):
    conv, act, taps = conv_out[0], act_grad[0], conv_kernel[0]
    shards = lax.axis_size("seq")
    groups = lax.axis_size("tensor")
    count = lax.axis_size("pipe")
    rank = sketch_matrix.shape[-1]
    after = lax.ppermute(
        jnp.concatenate([conv[:8], act[:8]], axis=0),
        "seq",
        [(i + 1, i) for i in range(shards - 1)],
    )
    both = front(conv, act, taps, layer_input[0])
    gathered = lax.all_gather(both, "seq", axis=0)
    row_terms, edge = edge_and_rows(conv, act, after, taps, both, sketch_matrix[0])
    row_terms = lax.all_to_all(row_terms.reshape(groups, -1, rank), "tensor", 0, 0, tiled=True)
    rows = jnp.sum(row_terms, axis=0).astype(B)
    share = rows.shape[0]
    small = lax.all_gather(jnp.concatenate([rows, edge], axis=0), "seq", axis=0)
    rows, edges = small[:, :share], small[:, share:]
    rows = lax.all_to_all(
        jnp.broadcast_to(rows[None], (groups,) + rows.shape), "tensor", 0, 0, tiled=True
    )
    gathered, rows, edges = lax.optimization_barrier((gathered, rows, edges))
    sketch, gram, terms = middle(gathered, rows, edges, in_proj[0])
    input_grad = lax.psum_scatter(terms, "tensor", scatter_dimension=0, tiled=True)
    gram = lax.all_to_all(gram.reshape(groups, -1, 128), "tensor", 0, 0, tiled=True)
    gram = lax.all_gather(jnp.sum(gram, axis=0), "tensor", axis=0, tiled=True)
    part = factored(gram, rank)
    input_grad, part = lax.optimization_barrier((input_grad, part))
    passed = lax.ppermute(input_grad, "pipe", [(i, (i - 1) % count) for i in range(count)])
    basis = applied(part, sketch, math.sqrt(D))
    return (passed[None], basis[None])


def solution(mesh):
    placed = (
        P("pipe", "seq", "tensor"),
        P("pipe", "seq", "tensor"),
        P("pipe", "seq", "tensor"),
        P("pipe", None, "tensor"),
        P("pipe", "seq", "tensor"),
        P("pipe", "tensor", None),
    )
    return jax.shard_map(
        local,
        mesh=mesh,
        in_specs=placed,
        out_specs=(P("pipe", "tensor", "seq"), P("pipe", "tensor", None)),
        check_vma=False,
    )
```

time: 475 us -> 211 us (0.44)
  the two profiles are of different devices: /device:TPU:26 before, /device:TPU:1 now
where the time goes in v2:
time: 211 us; the launch traced here: 210 us
  blocking collectives  87.1 us (41%)
  waiting for transfers between devices  45.8 us (22%)
  Pallas kernels  41.7 us (20%)
  starting transfers between devices  14.9 us (7%)
  between operations  14.1 us (7%)
  local copies, waits for them, and re-layouts  5.61 us (3%)
    all_gather x1, blocking collectives, local(): small = lax.all_gather(jnp.concatenate([rows, edge], axis=0), 'seq', axis=0)  39.9 us
    all_to_all x1, waiting for transfers between devices, local(): lax.all_to_all(jnp.broadcast_to(rows[None], (groups,) + rows.shape), 'ten...  25.5 us
    all_to_all x1, blocking collectives, local(): lax.all_to_all(row_terms.reshape(groups, -1, rank), 'tensor', 0, 0, tiled...  16.8 us
    all_gather x1, waiting for transfers between devices, local(): gathered = lax.all_gather(both, 'seq', axis=0)  15.9 us
    all_to_all x1, blocking collectives, local(): lax.all_to_all(gram.reshape(groups, -1, 128), 'tensor', 0, 0, tiled=True)  15.8 us
    pallas_call x1, Pallas kernels, middle(): pl.pallas_call(middle_kernel, out_shape=(jax.ShapeDtypeStruct((width, ran...  14.6 us
    pallas_call x1, Pallas kernels, factored(): pl.pallas_call(functools.partial(factor_kernel, blocks, FIRST), out_shape...  14.6 us
    all_gather x1, blocking collectives, local(): gram = lax.all_gather(jnp.sum(gram, axis=0), 'tensor', axis=0, tiled=True)  14.6 us
  transfers between devices with their start and end apart: 5, of which 3 were waited for; matrix products, arithmetic and copies ran while one was open for 2% of the time, Pallas kernels for 12%

profile of v2, /device:TPU:1, one launch (start us, length us, event | category | flops | bytes accessed | tf_op | source)
XLA Modules:
  0.0 210.1 jit_solution(5657412997366344449)
XLA Ops:
  7.2 0.0 all-gather.4.cloned.1.call-start
  7.2 2.6 %shard_map.77.grad_ref = bf16[256,1024]{1,0:T(8,128)(2,1)} custom-call(bf16[128,1024]{1,0:T(8,128)(2,1)} %bitcast.19, bf16[128,1024]{1,0:T(8,128)(2,1)} %bitcast.21, bf16[4,1024]{1,0:T(4,128)(2,1)} %bitcast.30, bf16[128,1024]{1,0:T(8,128)(2,1)} %bitcast.27), custom_call_target="tpu_custom_call" | custom-call | tf_op jit(solution)/shard_map/pallas_call | solution.py:65
  9.8 0.7 slice_bitcast_fusion
  10.5 1.3 collective-permute-start
  11.8 4.4 %collective-permute-done.next_ref = bf16[16,1024]{1,0:T(8,128)(2,1)S(1)} collective-permute-done((bf16[16,1024]{1,0:T(8,128)(2,1)S(1)}, bf16[16,1024]{1,0:T(8,128)(2,1)S(1)}, u32[]{:S(2)}, u32[]{:S(2)}) %collective-permute-start) | collective-permute-done | bytes 32800 | tf_op jit(solution)/shard_map/ppermute | solution.py:377
  16.2 0.6 copy-done.3
  16.8 2.4 %shard_map.78 = (f32[128,512]{1,0:T(8,128)}, bf16[32,512]{1,0:T(8,128)(2,1)}) custom-call(bf16[128,1024]{1,0:T(8,128)(2,1)} %bitcast.20, bf16[128,1024]{1,0:T(8,128)(2,1)} %bitcast.22, bf16[16,1024]{1,0:T(8,128)(2,1)} %copy-done.3, bf16[4,1024]{1,0:T(4,128)(2,1)} %bitcast.31, bf16[256,1024]{1,0:T(8,128)(2,1)} %shard_map.77.grad_ref, bf16[1024,512]{1,0:T(8,128)(2,1)} %bitcast.24), custom_call_target="tpu_custom_call" | custom-call | tf_op jit(solution)/shard_map/pallas_call | solution.py:94
  19.2 16.8 %all_to_all.15 = f32[8,16,512]{2,1,0:T(8,128)S(1)} all-to-all(f32[8,16,512]{2,1,0:T(8,128)} %bitcast.29), channel_id=1, replica_groups=mesh['pipe'=4,'seq'=16,'tensor'=8] {'tensor'}, dimensions={0} | all-to-all | bytes 524288 | tf_op jit(solution)/shard_map/all_to_all | solution.py:385
  36.1 0.8 pad_maximum_fusion
  36.8 39.9 %all-gather.1 = bf16[768,512]{1,0:T(8,128)(2,1)S(1)} all-gather(bf16[48,512]{1,0:T(8,128)(2,1)S(1)} %pad_maximum_fusion), channel_id=3, replica_groups=mesh['pipe'=4,'seq'=16,'tensor'=8] {'seq'}, dimensions={0}, use_global_device_ids=true | all-gather | bytes 835584 | tf_op jit(solution)/shard_map/all_gather | solution.py:388
  76.8 1.6 broadcast_in_dim.12
  78.4 9.7 %all-to-all-start.1 = ((bf16[8,16,16,512]{3,2,1,0:T(8,128)(2,1)}), bf16[8,16,16,512]{3,2,1,0:T(8,128)(2,1)S(1)}, u32[]{:S(2)}, u32[]{:S(2)}) async-start(bf16[8,16,16,512]{3,2,1,0:T(8,128)(2,1)} %broadcast_in_dim.12), calls=%async_computation.1 | async-start | bytes 4194304 | tf_op jit(solution)/shard_map/all_to_all | solution.py:390
  88.1 0.9 slice.25.edge_ref
  89.0 25.5 %all-to-all-done.1.rows_ref = bf16[8,16,16,512]{3,2,1,0:T(8,128)(2,1)S(1)} async-done(((bf16[8,16,16,512]{3,2,1,0:T(8,128)(2,1)}), bf16[8,16,16,512]{3,2,1,0:T(8,128)(2,1)S(1)}, u32[]{:S(2)}, u32[]{:S(2)}) %all-to-all-start.1) | async-done | bytes 2097184 | tf_op jit(solution)/shard_map/all_to_all | solution.py:390
  114.5 15.9 %all-gather.4.cloned.1.call-done = bf16[4096,1024]{1,0:T(8,128)(2,1)} async-done(((bf16[256,1024]{1,0:T(8,128)(2,1)}), bf16[4096,1024]{1,0:T(8,128)(2,1)}) %all-gather.4.cloned.1.call-update) | async-done | bytes 8388624 | tf_op jit(solution)/shard_map/all_gather | solution.py:383
  130.4 14.6 %shard_map.79 = (f32[1024,512]{1,0:T(8,128)}, f32[1280,128]{1,0:T(8,128)}, bf16[2048,512]{1,0:T(8,128)(2,1)}) custom-call(bf16[16,256,1024]{2,1,0:T(8,128)(2,1)} %bitcast.16, bf16[8,16,16,512]{3,2,1,0:T(8,128)(2,1)} %copy-done.1, bf16[16,32,512]{2,1,0:T(8,128)(2,1)} %slice.25.edge_ref, bf16[512,1024]{1,0:T(8,128)(2,1)} %bitcast.23), custom_call_target="tpu_custom_call" | custom-call | tf_op jit(solution)/shard_map/pallas_call | solution.py:194
  145.0 1.1 copy-done.2
  146.1 15.8 %all_to_all.16 = f32[8,160,128]{2,1,0:T(8,128)S(1)} all-to-all(f32[8,160,128]{2,1,0:T(8,128)S(1)} %bitcast.26), channel_id=1, replica_groups=mesh['pipe'=4,'seq'=16,'tensor'=8] {'tensor'}, dimensions={0} | all-to-all | bytes 1310720 | tf_op jit(solution)/shard_map/all_to_all | solution.py:396
  161.9 14.6 %all_gather.19.gram_ref = f32[1280,128]{1,0:T(8,128)S(1)} all-gather(f32[160,128]{1,0:T(8,128)S(1)} %reduce_sum.19), channel_id=1, replica_groups=mesh['pipe'=4,'seq'=16,'tensor'=8] {'tensor'}, dimensions={0}, use_global_device_ids=true | all-gather | bytes 737280 | tf_op jit(solution)/shard_map/all_gather | solution.py:397
  176.4 14.6 %shard_map.80.part_ref = f32[512,512]{1,0:T(8,128)S(1)} custom-call(f32[1280,128]{1,0:T(8,128)S(1)} %all_gather.19.gram_ref), custom_call_target="tpu_custom_call" | custom-call | tf_op jit(solution)/shard_map/pallas_call | solution.py:345
  191.1 0.0 reduce-scatter.2.cloned.1.call-done
  191.1 3.9 %collective-permute-start.1 = (bf16[256,512]{1,0:T(8,128)(2,1)}, bf16[256,512]{1,0:T(8,128)(2,1)S(1)}, u32[]{:S(2)}, u32[]{:S(2)}) collective-permute-start(bf16[256,512]{1,0:T(8,128)(2,1)} %reduce-scatter.2.cloned.1.call-done), channel_id=1, source_target_pairs={{0,384},{128,0},{256,128},{384,256},{1,385},{129,1},{257,129},{385... | collective-permute-start | bytes 786440 | tf_op jit(solution)/shard_map/ppermute | solution.py:400
  195.0 7.5 %shard_map.81 = bf16[1024,512]{1,0:T(8,128)(2,1)} custom-call(f32[512,512]{1,0:T(8,128)S(1)} %shard_map.80.part_ref, f32[1024,512]{1,0:T(8,128)S(1)} %copy-done), custom_call_target="tpu_custom_call" | custom-call | tf_op jit(solution)/shard_map/pallas_call | solution.py:357
  202.5 0.7 copy.9
  (14 shorter events, 0.1 us)
Async XLA Ops:
  7.2 123.2 %all-gather.4.cloned.1.call-start = ((), (), s32[]{:S(2)}) async-start(), calls=%async_computation.5 | async-start | bytes 8912896 | tf_op jit(solution)/shard_map/all_gather | solution.py:383
  10.5 5.7 %collective-permute-start = (bf16[16,1024]{1,0:T(8,128)(2,1)S(1)}, bf16[16,1024]{1,0:T(8,128)(2,1)S(1)}, u32[]{:S(2)}, u32[]{:S(2)}) collective-permute-start(bf16[16,1024]{1,0:T(8,128)(2,1)S(1)} %pad_maximum_fusion.1), channel_id=1, source_target_pairs={{8,0},{16,8},{24,16},{32,24},{40,32},{48,40},{56,48},{64,56},{72,6... | collective-permute-start | bytes 98312 | tf_op jit(solution)/shard_map/ppermute | solution.py:377
  16.2 0.6 copy-start.3
  78.4 36.0 %all-to-all-start.1 = ((bf16[8,16,16,512]{3,2,1,0:T(8,128)(2,1)}), bf16[8,16,16,512]{3,2,1,0:T(8,128)(2,1)S(1)}, u32[]{:S(2)}, u32[]{:S(2)}) async-start(bf16[8,16,16,512]{3,2,1,0:T(8,128)(2,1)} %broadcast_in_dim.12), calls=%async_computation.1 | async-start | bytes 4194304 | tf_op jit(solution)/shard_map/all_to_all | solution.py:390
  88.1 103.0 %reduce-scatter.2.cloned.1.call-start = ((), (), s32[]{:S(2)}) async-start(), calls=%async_computation.4 | async-start | bytes 2359296 | tf_op jit(solution)/shard_map/reduce_scatter | solution.py:395
  114.5 15.9 %copy-start.1 = (bf16[8,16,16,512]{3,2,1,0:T(8,128)(2,1)}, bf16[8,16,16,512]{3,2,1,0:T(8,128)(2,1)S(1)}, u32[]{:S(2)}) copy-start(bf16[8,16,16,512]{3,2,1,0:T(8,128)(2,1)S(1)} %all-to-all-done.1.rows_ref) | copy-start | bytes 6291460
  145.0 1.1 copy-start.2
  146.1 49.0 %copy-start = (f32[1024,512]{1,0:T(8,128)S(1)}, f32[1024,512]{1,0:T(8,128)}, u32[]{:S(2)}) copy-start(f32[1024,512]{1,0:T(8,128)} %get-tuple-element.21.sketch_ref) | copy-start | bytes 6291460
  191.1 11.4 %collective-permute-start.1 = (bf16[256,512]{1,0:T(8,128)(2,1)}, bf16[256,512]{1,0:T(8,128)(2,1)S(1)}, u32[]{:S(2)}, u32[]{:S(2)}) collective-permute-start(bf16[256,512]{1,0:T(8,128)(2,1)} %reduce-scatter.2.cloned.1.call-done), channel_id=1, source_target_pairs={{0,384},{128,0},{256,128},{384,256},{1,385},{129,1},{257,129},{385... | collective-permute-start | bytes 786440 | tf_op jit(solution)/shard_map/ppermute | solution.py:400
Sparse Core Ops, SparseCore 0:
  10.7 119.6 all-gather.3
  145.1 38.6 reduce-scatter.1

commit v3 on v2

--- a/solution.py
+++ b/solution.py
@@ -16,6 +16,7 @@
 ANY = pl.BlockSpec(memory_space=pl.ANY)
 LIMIT = 32 * 1024 * 1024
 WIDE = 58 * 1024 * 1024
+MOST = 56 * 1024 * 1024
 EDGE = 16
 
 
@@ -76,8 +77,8 @@
     held[EDGE : EDGE + 8, :] = pre_grad(after[0:8, :], after[8:16, :])
     edge = convolved(held, taps_ref[...].astype(F), EDGE)
     half = edge.shape[1] // 2
-    edge_ref[0:EDGE, :] = edge[:, 0:half]
-    edge_ref[EDGE : 2 * EDGE, :] = edge[:, half:]
+    wide = edge.astype(F)
+    edge_ref[...] = jnp.concatenate([wide[8:EDGE, half:], wide[8:EDGE, 0:half]], axis=0).astype(B)
     rows = grad_ref.shape[0]
     grad = jnp.concatenate([grad_ref[0 : rows - EDGE, :], edge], axis=0)
     rows_ref[...] = jnp.dot(grad, test_ref[...], preferred_element_type=F)
@@ -96,7 +97,7 @@
         grid=(1,),
         out_shape=(
             jax.ShapeDtypeStruct((rows, rank), F),
-            jax.ShapeDtypeStruct((2 * EDGE, width // 2), B),
+            jax.ShapeDtypeStruct((EDGE, width // 2), B),
         ),
         in_specs=[
             pl.BlockSpec((EDGE, width), lambda i: (last, 0)),
@@ -106,24 +107,21 @@
             pl.BlockSpec((rows, width), lambda i: (1, 0)),
             whole(*test.shape),
         ],
-        out_specs=(whole(rows, rank), whole(2 * EDGE, width // 2)),
+        out_specs=(whole(rows, rank), whole(EDGE, width // 2)),
         scratch_shapes=[pltpu.VMEM((EDGE + 8, width), F)],
         compiler_params=pltpu.CompilerParams(vmem_limit_bytes=WIDE),
     )(conv, act, after, taps, both, test)
 
 
-CHUNKS = 4
-
-
 def middle_kernel(
     both_ref, rows_ref, edge_ref, weight_ref, sketch_ref, gram_ref, terms_ref,
-    acts, grads, terms, right_all, weights, in_sems, out_sems,
+    acts, grads, terms, right, weights, sketch, gram, in_sems, out_sems,
 ):
     shards, twice, width = both_ref.shape
     tokens = twice // 2
     groups, _, share, rank = rows_ref.shape
-    cols = width // CHUNKS
-    each = shards // CHUNKS
+    chunks, each = grads.shape[:2]
+    cols = width // chunks
 
     def acts_copy(i):
         return pltpu.make_async_copy(
@@ -132,7 +130,7 @@
 
     def grads_copy(i):
         return pltpu.make_async_copy(
-            both_ref.at[i * each : (i + 1) * each, tokens:twice, :], grads.at[i], in_sems.at[CHUNKS + i]
+            both_ref.at[i * each : (i + 1) * each, tokens:twice, :], grads.at[i], in_sems.at[chunks + i]
         )
 
     def terms_copy(i):
@@ -140,46 +138,61 @@
             terms.at[i], terms_ref.at[i * each * tokens : (i + 1) * each * tokens, :], out_sems.at[i]
         )
 
-    rows_copy = pltpu.make_async_copy(rows_ref, right_all, in_sems.at[2 * CHUNKS])
-    weight_copy = pltpu.make_async_copy(weight_ref, weights, in_sems.at[2 * CHUNKS + 1])
-    acts_copy(0).start()
-    rows_copy.start()
-    for i in range(1, CHUNKS):
+    def rows_copy(g):
+        return pltpu.make_async_copy(
+            rows_ref.at[g], right.at[:, g * share : (g + 1) * share, :], in_sems.at[2 * chunks + 1 + g]
+        )
+
+    def sketch_copy(i):
+        at = slice(i * cols, (i + 1) * cols)
+        return pltpu.make_async_copy(sketch.at[at, :], sketch_ref.at[at, :], out_sems.at[chunks + i])
+
+    weight_copy = pltpu.make_async_copy(weight_ref, weights, in_sems.at[2 * chunks])
+    gram_copy = pltpu.make_async_copy(gram, gram_ref, out_sems.at[2 * chunks])
+    for g in range(groups):
+        rows_copy(g).start()
+    for i in range(chunks):
         acts_copy(i).start()
     weight_copy.start()
-    for i in range(CHUNKS):
+    for i in range(chunks):
         grads_copy(i).start()
-    rows_copy.wait()
-    for i in range(CHUNKS):
+    for g in range(groups):
+        rows_copy(g).wait()
+    for i in range(chunks):
         acts_copy(i).wait()
-        part = jnp.zeros((cols, rank), F)
-        for g in range(groups):
-            left = acts[i, :, g * share : (g + 1) * share, :].reshape(shards * share, cols)
-            right = right_all[g].reshape(shards * share, rank)
-            part += dot(left, right, 0, 0, None)
-        sketch_ref[i * cols : (i + 1) * cols, :] = part
+        left = acts[i].reshape(shards * tokens, cols)
+        part = dot(left, right[...].reshape(shards * tokens, rank), 0, 0, None)
+        sketch[i * cols : (i + 1) * cols, :] = part
+        sketch_copy(i).start()
         at = 0
         for r in range(rank // 128):
             block = dot(part[:, r * 128 : (r + 1) * 128], part[:, r * 128 :], 0, 0)
             for c in range(block.shape[1] // 128):
                 piece = block[:, c * 128 : (c + 1) * 128]
                 if i == 0:
-                    gram_ref[at : at + 128, :] = piece
+                    gram[at : at + 128, :] = piece
                 else:
-                    gram_ref[at : at + 128, :] += piece
+                    gram[at : at + 128, :] += piece
                 at += 128
+    gram_copy.start()
     half = width // 2
+    final = lax.broadcasted_iota(jnp.int32, (EDGE, half), 0) >= 8
     weight_copy.wait()
-    for i in range(CHUNKS):
+    for i in range(chunks):
         grads_copy(i).wait()
         for z in range(each):
-            edge = edge_ref[i * each + z]
-            grads[i, z, tokens - EDGE : tokens, 0:half] = edge[0:EDGE, :]
-            grads[i, z, tokens - EDGE : tokens, half:] = edge[EDGE : 2 * EDGE, :]
+            edge = edge_ref[i * each + z].astype(F)
+            other = jnp.concatenate([edge[8:EDGE, :], edge[0:8, :]], axis=0)
+            old = grads[i, z, tokens - EDGE : tokens, :].astype(F)
+            new = [jnp.where(final, edge, old[:, 0:half]), jnp.where(final, other, old[:, half:])]
+            grads[i, z, tokens - EDGE : tokens, :] = jnp.concatenate(new, axis=1).astype(B)
         left = grads[i].reshape(each * tokens, width)
         terms[i] = dot(left, weights[...], 1, 1, None).astype(B)
         terms_copy(i).start()
-    for i in range(CHUNKS):
+    for i in range(chunks):
+        sketch_copy(i).wait()
+    gram_copy.wait()
+    for i in range(chunks):
         terms_copy(i).wait()
 
 
@@ -190,7 +203,8 @@
     blocks = rank // 128
     packed = blocks * (blocks + 1) // 2 * 128
     outs = weights.shape[0]
-    each = shards // CHUNKS
+    chunks = 4
+    each = shards // chunks
     return pl.pallas_call(
         middle_kernel,
         out_shape=(
@@ -199,17 +213,19 @@
             jax.ShapeDtypeStruct((shards * tokens, outs), B),
         ),
         in_specs=[ANY, ANY, VMEM, ANY],
-        out_specs=(VMEM, VMEM, ANY),
+        out_specs=(ANY, ANY, ANY),
         scratch_shapes=[
-            pltpu.VMEM((CHUNKS, shards, tokens, width // CHUNKS), B),
-            pltpu.VMEM((CHUNKS, each, tokens, width), B),
-            pltpu.VMEM((CHUNKS, each * tokens, outs), B),
-            pltpu.VMEM(rows.shape, B),
+            pltpu.VMEM((chunks, shards, tokens, width // chunks), B),
+            pltpu.VMEM((chunks, each, tokens, width), B),
+            pltpu.VMEM((chunks, each * tokens, outs), B),
+            pltpu.VMEM((shards, tokens, rank), B),
             pltpu.VMEM(weights.shape, B),
-            pltpu.SemaphoreType.DMA((2 * CHUNKS + 2,)),
-            pltpu.SemaphoreType.DMA((CHUNKS,)),
+            pltpu.VMEM((width, rank), F),
+            pltpu.VMEM((packed, 128), F),
+            pltpu.SemaphoreType.DMA((2 * chunks + 1 + rows.shape[0],)),
+            pltpu.SemaphoreType.DMA((2 * chunks + 1,)),
         ],
-        compiler_params=pltpu.CompilerParams(vmem_limit_bytes=WIDE),
+        compiler_params=pltpu.CompilerParams(vmem_limit_bytes=MOST),
     )(gathered, rows, edges, weights)
 
 

time: 211 us -> 206 us (0.976)
  blocking collectives: 87.1 us -> 118 us
  waiting for transfers between devices: 45.8 us -> 23.5 us
  starting transfers between devices: 14.9 us -> 5.25 us
    all_to_all x0 -> x1, blocking collectives: none -> 35 us  [local(): lax.all_to_all(jnp.broadcast_to(rows[None], (groups,) + rows.shape), 'ten...]
    all_to_all x1 -> x0, waiting for transfers between devices: 25.5 us -> none  [local(): lax.all_to_all(jnp.broadcast_to(rows[None], (groups,) + rows.shape), 'ten...]
    all_to_all x1 -> x0, starting transfers between devices: 9.69 us -> none  [local(): lax.all_to_all(jnp.broadcast_to(rows[None], (groups,) + rows.shape), 'ten...]
    all_gather x1, blocking collectives: 39.9 us -> 35.6 us  [local(): small = lax.all_gather(jnp.concatenate([rows, edge], axis=0), 'seq', axis=0)]
    all_gather x1, waiting for transfers between devices: 15.9 us -> 19.1 us  [local(): gathered = lax.all_gather(both, 'seq', axis=0)]
  transfers between devices with their start and end apart: 5 -> 4, of which waited for: 3 -> 2; matrix products, arithmetic and copies ran while one was open for 2% -> 1% of each run, Pallas kernels for 12% -> 12%
where the time goes in v3:
time: 206 us
  blocking collectives  118 us (57%)
  Pallas kernels  40.1 us (19%)
  waiting for transfers between devices  23.5 us (11%)
  between operations  14.1 us (7%)
  starting transfers between devices  5.25 us (3%)
  local copies, waits for them, and re-layouts  4.11 us (2%)
    all_gather x1, blocking collectives, local(): small = lax.all_gather(jnp.concatenate([rows, edge], axis=0), 'seq', axis=0)  35.6 us
    all_to_all x1, blocking collectives, local(): lax.all_to_all(jnp.broadcast_to(rows[None], (groups,) + rows.shape), 'ten...  35 us
    all_gather x1, waiting for transfers between devices, local(): gathered = lax.all_gather(both, 'seq', axis=0)  19.1 us
    all_to_all x1, blocking collectives, local(): lax.all_to_all(row_terms.reshape(groups, -1, rank), 'tensor', 0, 0, tiled...  16.8 us
    all_to_all x1, blocking collectives, local(): lax.all_to_all(gram.reshape(groups, -1, 128), 'tensor', 0, 0, tiled=True)  15.8 us
    pallas_call x1, Pallas kernels, factored(): pl.pallas_call(functools.partial(factor_kernel, blocks, FIRST), out_shape...  14.6 us
    all_gather x1, blocking collectives, local(): gram = lax.all_gather(jnp.sum(gram, axis=0), 'tensor', axis=0, tiled=True)  14.6 us
    pallas_call x1, Pallas kernels, middle(): pl.pallas_call(middle_kernel, out_shape=(jax.ShapeDtypeStruct((width, ran...  13 us
  transfers between devices with their start and end apart: 4, of which 2 were waited for; matrix products, arithmetic and copies ran while one was open for 1% of the time, Pallas kernels for 12%

profile of v3, /device:TPU:1, one launch (start us, length us, event | category | flops | bytes accessed | tf_op | source)
XLA Modules:
  0.0 205.7 jit_solution(291543207966825642)
XLA Ops:
  7.2 0.0 all-gather.4.cloned.1.call-start
  7.2 2.6 %shard_map.77.grad_ref = bf16[256,1024]{1,0:T(8,128)(2,1)} custom-call(bf16[128,1024]{1,0:T(8,128)(2,1)} %bitcast.18, bf16[128,1024]{1,0:T(8,128)(2,1)} %bitcast.20, bf16[4,1024]{1,0:T(4,128)(2,1)} %bitcast.29, bf16[128,1024]{1,0:T(8,128)(2,1)} %bitcast.26), custom_call_target="tpu_custom_call" | custom-call | tf_op jit(solution)/shard_map/pallas_call | solution.py:66
  9.8 0.0 reduce-scatter.2.cloned.1.call-start
  9.9 0.7 slice_bitcast_fusion
  10.6 1.3 collective-permute-start
  11.9 4.4 %collective-permute-done.next_ref = bf16[16,1024]{1,0:T(8,128)(2,1)S(1)} collective-permute-done((bf16[16,1024]{1,0:T(8,128)(2,1)S(1)}, bf16[16,1024]{1,0:T(8,128)(2,1)S(1)}, u32[]{:S(2)}, u32[]{:S(2)}) %collective-permute-start) | collective-permute-done | bytes 32800 | tf_op jit(solution)/shard_map/ppermute | solution.py:393
  16.3 0.6 copy-done.2
  16.9 2.4 %shard_map.78 = (f32[128,512]{1,0:T(8,128)}, bf16[16,512]{1,0:T(8,128)(2,1)}) custom-call(bf16[128,1024]{1,0:T(8,128)(2,1)} %bitcast.19, bf16[128,1024]{1,0:T(8,128)(2,1)} %bitcast.21, bf16[16,1024]{1,0:T(8,128)(2,1)} %copy-done.2, bf16[4,1024]{1,0:T(4,128)(2,1)} %bitcast.30, bf16[256,1024]{1,0:T(8,128)(2,1)} %shard_map.77.grad_ref, bf16[1024,512]{1,0:T(8,128)(2,1)} %bitcast.23), custom_call_target="tpu_custom_call" | custom-call | tf_op jit(solution)/shard_map/pallas_call | solution.py:95
  19.3 16.8 %all_to_all.15 = f32[8,16,512]{2,1,0:T(8,128)S(1)} all-to-all(f32[8,16,512]{2,1,0:T(8,128)} %bitcast.28), channel_id=1, replica_groups=mesh['pipe'=4,'seq'=16,'tensor'=8] {'tensor'}, dimensions={0} | all-to-all | bytes 524288 | tf_op jit(solution)/shard_map/all_to_all | solution.py:401
  36.1 0.7 pad_maximum_fusion.1
  36.9 35.6 %all-gather.1 = bf16[512,512]{1,0:T(8,128)(2,1)S(1)} all-gather(bf16[32,512]{1,0:T(8,128)(2,1)S(1)} %pad_maximum_fusion.1), channel_id=3, replica_groups=mesh['pipe'=4,'seq'=16,'tensor'=8] {'seq'}, dimensions={0}, use_global_device_ids=true | all-gather | bytes 557056 | tf_op jit(solution)/shard_map/all_gather | solution.py:404
  72.5 0.7 fusion
  73.2 0.3 broadcast_in_dim.12
  73.5 35.0 %all_to_all.16.rows_ref = bf16[8,16,16,512]{3,2,1,0:T(8,128)(2,1)} all-to-all(bf16[8,16,16,512]{3,2,1,0:T(8,128)(2,1)S(1)} %broadcast_in_dim.12), channel_id=1, replica_groups=mesh['pipe'=4,'seq'=16,'tensor'=8] {'tensor'}, dimensions={0} | all-to-all | bytes 4194304 | tf_op jit(solution)/shard_map/all_to_all | solution.py:406
  108.5 19.1 %all-gather.4.cloned.1.call-done = bf16[4096,1024]{1,0:T(8,128)(2,1)} async-done(((bf16[256,1024]{1,0:T(8,128)(2,1)}), bf16[4096,1024]{1,0:T(8,128)(2,1)}) %all-gather.4.cloned.1.call-update) | async-done | bytes 8388624 | tf_op jit(solution)/shard_map/all_gather | solution.py:399
  127.5 13.0 %shard_map.79 = (f32[1024,512]{1,0:T(8,128)}, f32[1280,128]{1,0:T(8,128)}, bf16[2048,512]{1,0:T(8,128)(2,1)}) custom-call(bf16[16,256,1024]{2,1,0:T(8,128)(2,1)} %bitcast.16, bf16[8,16,16,512]{3,2,1,0:T(8,128)(2,1)} %all_to_all.16.rows_ref, bf16[16,16,512]{2,1,0:T(8,128)(2,1)} %get-tuple-element.16.edge_ref, bf16[512,1024]{1,0:T(8,128)(2,1)} %bitcast.22), custom_call_target="tpu_custom_call" | custom-call | tf_op jit(solution)/shard_map/pallas_call | solution.py:208
  140.6 1.1 copy-done.1
  141.7 15.8 %all_to_all.17 = f32[8,160,128]{2,1,0:T(8,128)S(1)} all-to-all(f32[8,160,128]{2,1,0:T(8,128)S(1)} %bitcast.25), channel_id=1, replica_groups=mesh['pipe'=4,'seq'=16,'tensor'=8] {'tensor'}, dimensions={0} | all-to-all | bytes 1310720 | tf_op jit(solution)/shard_map/all_to_all | solution.py:412
  157.5 14.6 %all_gather.19.gram_ref = f32[1280,128]{1,0:T(8,128)S(1)} all-gather(f32[160,128]{1,0:T(8,128)S(1)} %reduce_sum.19), channel_id=1, replica_groups=mesh['pipe'=4,'seq'=16,'tensor'=8] {'tensor'}, dimensions={0}, use_global_device_ids=true | all-gather | bytes 737280 | tf_op jit(solution)/shard_map/all_gather | solution.py:413
  172.1 14.6 %shard_map.80.part_ref = f32[512,512]{1,0:T(8,128)S(1)} custom-call(f32[1280,128]{1,0:T(8,128)S(1)} %all_gather.19.gram_ref), custom_call_target="tpu_custom_call" | custom-call | tf_op jit(solution)/shard_map/pallas_call | solution.py:361
  186.7 0.0 reduce-scatter.2.cloned.1.call-done
  186.8 3.9 %collective-permute-start.1 = (bf16[256,512]{1,0:T(8,128)(2,1)}, bf16[256,512]{1,0:T(8,128)(2,1)S(1)}, u32[]{:S(2)}, u32[]{:S(2)}) collective-permute-start(bf16[256,512]{1,0:T(8,128)(2,1)} %reduce-scatter.2.cloned.1.call-done), channel_id=1, source_target_pairs={{0,384},{128,0},{256,128},{384,256},{1,385},{129,1},{257,129},{385... | collective-permute-start | bytes 786440 | tf_op jit(solution)/shard_map/ppermute | solution.py:416
  190.7 7.5 %shard_map.81 = bf16[1024,512]{1,0:T(8,128)(2,1)} custom-call(f32[512,512]{1,0:T(8,128)S(1)} %shard_map.80.part_ref, f32[1024,512]{1,0:T(8,128)S(1)} %copy-done), custom_call_target="tpu_custom_call" | custom-call | tf_op jit(solution)/shard_map/pallas_call | solution.py:373
  198.1 0.7 copy.9
  (10 shorter events, 0.1 us)
Async XLA Ops:
  7.2 120.4 %all-gather.4.cloned.1.call-start = ((), (), s32[]{:S(2)}) async-start(), calls=%async_computation.5 | async-start | bytes 8912896 | tf_op jit(solution)/shard_map/all_gather | solution.py:399
  9.8 176.9 %reduce-scatter.2.cloned.1.call-start = ((), (), s32[]{:S(2)}) async-start(), calls=%async_computation.4 | async-start | bytes 2359296 | tf_op jit(solution)/shard_map/reduce_scatter | solution.py:411
  10.6 5.7 %collective-permute-start = (bf16[16,1024]{1,0:T(8,128)(2,1)S(1)}, bf16[16,1024]{1,0:T(8,128)(2,1)S(1)}, u32[]{:S(2)}, u32[]{:S(2)}) collective-permute-start(bf16[16,1024]{1,0:T(8,128)(2,1)S(1)} %pad_maximum_fusion), channel_id=1, source_target_pairs={{8,0},{16,8},{24,16},{32,24},{40,32},{48,40},{56,48},{64,56},{72,6... | collective-permute-start | bytes 98312 | tf_op jit(solution)/shard_map/ppermute | solution.py:393
  16.3 0.6 copy-start.2
  140.6 1.1 copy-start.1
  141.7 49.0 %copy-start = (f32[1024,512]{1,0:T(8,128)S(1)}, f32[1024,512]{1,0:T(8,128)}, u32[]{:S(2)}) copy-start(f32[1024,512]{1,0:T(8,128)} %get-tuple-element.21.sketch_ref) | copy-start | bytes 6291460
  186.8 11.4 %collective-permute-start.1 = (bf16[256,512]{1,0:T(8,128)(2,1)}, bf16[256,512]{1,0:T(8,128)(2,1)S(1)}, u32[]{:S(2)}, u32[]{:S(2)}) collective-permute-start(bf16[256,512]{1,0:T(8,128)(2,1)} %reduce-scatter.2.cloned.1.call-done), channel_id=1, source_target_pairs={{0,384},{128,0},{256,128},{384,256},{1,385},{129,1},{257,129},{385... | collective-permute-start | bytes 786440 | tf_op jit(solution)/shard_map/ppermute | solution.py:416
Sparse Core Ops, SparseCore 0:
  10.7 116.8 all-gather.3
  140.8 38.6 reduce-scatter.1

commit v4 on v3

--- a/solution.py
+++ b/solution.py
@@ -63,10 +63,18 @@
 
 def front(conv, act, taps, acts):
     rows, width = conv.shape
+    part = width // 2
+
+    def columns(count):
+        return pl.BlockSpec((count, part), lambda i: (0, i))
+
     return pl.pallas_call(
         front_kernel,
+        grid=(width // part,),
         out_shape=jax.ShapeDtypeStruct((2 * rows, width), B),
-        scratch_shapes=[pltpu.VMEM((rows + 8, width), F)],
+        in_specs=[columns(rows), columns(rows), columns(taps.shape[0]), columns(rows)],
+        out_specs=columns(2 * rows),
+        scratch_shapes=[pltpu.VMEM((rows + 8, part), F)],
         compiler_params=pltpu.CompilerParams(vmem_limit_bytes=WIDE),
     )(conv, act, taps, acts)
 
@@ -300,17 +308,24 @@
     work[:, 0:128] = m[pl.ds(base, 128), pl.ds(base, 128)]
     work[:, 128:256] = eye
     leaf(work, staged)
-    m[pl.ds(base, 128), pl.ds(base, 128)] = eye
-    m[pl.ds(base, 128), :] = dot(work[:, 128:256], m[pl.ds(base, 128), :], 1, 0)
-
-    def update(j, carry):
-        at = pl.multiple_of(j * 128, 128)
-        factor = m[pl.ds(base, 128), pl.ds(at, 128)]
-        m[pl.ds(at, 128), pl.ds(base, 128)] = jnp.zeros((128, 128), F)
-        m[pl.ds(at, 128), :] -= dot(factor, m[pl.ds(base, 128), :], 0, 0)
-        return carry
-
-    lax.fori_loop(k + 1, blocks, update, 0)
+    width = blocks * 128
+
+    def eliminate(top):
+        end = top + 128
+        inv = work[:, 128:256]
+        if top > 0:
+            m[top:end, 0:top] = dot(inv, m[top:end, 0:top], 1, 0)
+        m[top:end, top:end] = inv
+        if end < width:
+            m[top:end, end:width] = dot(inv, m[top:end, end:width], 1, 0)
+            change = dot(m[top:end, end:width], m[top:end, :], 0, 0)
+            if top > 0:
+                m[end:width, 0:top] -= change[:, 0:top]
+            m[end:width, top:end] = -change[:, top:end]
+            m[end:width, end:width] -= change[:, end:width]
+
+    for which in range(blocks):
+        pl.when(k == which)(functools.partial(eliminate, which * 128))
 
 
 def factor_kernel(blocks, stages, gram_ref, m, work, staged):
@@ -341,13 +356,18 @@
     for r in range(blocks):
         for c in range(r + 1, blocks):
             m[r * 128 : (r + 1) * 128, c * 128 : (c + 1) * 128] = jnp.zeros((128, 128), F)
+    rank = blocks * 128
     inv_hi, inv_lo = split(m[...] * scale)
 
     def rows(i, carry):
         at = pl.multiple_of(i * 256, 256)
         hi, lo = split(sketch_ref[pl.ds(at, 256), :])
-        out = dot(hi, inv_hi, 1, 1, None) + (dot(hi, inv_lo, 1, 1, None) + dot(lo, inv_hi, 1, 1, None))
-        out_ref[pl.ds(at, 256), :] = out.astype(B)
+        for c in range(0, rank, 256):
+            end = min(c + 256, rank)
+            left, right = inv_hi[c:end, 0:end], inv_lo[c:end, 0:end]
+            out = dot(hi[:, 0:end], left, 1, 1, None)
+            out += dot(hi[:, 0:end], right, 1, 1, None) + dot(lo[:, 0:end], left, 1, 1, None)
+            out_ref[pl.ds(at, 256), c:end] = out.astype(B)
         return carry
 
     lax.fori_loop(0, sketch_ref.shape[0] // 256, rows, 0)

time: 206 us -> 205 us (level)
  transfers between devices with their start and end apart: 4 -> 4, of which waited for: 2 -> 2; matrix products, arithmetic and copies ran while one was open for 1% -> 1% of each run, Pallas kernels for 12% -> 11%
where the time goes in v4:
time: 205 us; the launch traced here: 204 us
  blocking collectives  118 us (58%)
  Pallas kernels  38.3 us (19%)
  waiting for transfers between devices  23.7 us (12%)
  between operations  14.1 us (7%)
  starting transfers between devices  5.25 us (3%)
  local copies, waits for them, and re-layouts  4.11 us (2%)
    all_gather x1, blocking collectives, local(): small = lax.all_gather(jnp.concatenate([rows, edge], axis=0), 'seq', axis=0)  35.6 us
    all_to_all x1, blocking collectives, local(): lax.all_to_all(jnp.broadcast_to(rows[None], (groups,) + rows.shape), 'ten...  35 us
    all_gather x1, waiting for transfers between devices, local(): gathered = lax.all_gather(both, 'seq', axis=0)  19.3 us
    all_to_all x1, blocking collectives, local(): lax.all_to_all(row_terms.reshape(groups, -1, rank), 'tensor', 0, 0, tiled...  16.8 us
    all_to_all x1, blocking collectives, local(): lax.all_to_all(gram.reshape(groups, -1, 128), 'tensor', 0, 0, tiled=True)  15.8 us
    all_gather x1, blocking collectives, local(): gram = lax.all_gather(jnp.sum(gram, axis=0), 'tensor', axis=0, tiled=True)  14.6 us
    pallas_call x1, Pallas kernels, factored(): pl.pallas_call(functools.partial(factor_kernel, blocks, FIRST), out_shape...  13.5 us
    pallas_call x1, Pallas kernels, middle(): pl.pallas_call(middle_kernel, out_shape=(jax.ShapeDtypeStruct((width, ran...  13 us
  transfers between devices with their start and end apart: 4, of which 2 were waited for; matrix products, arithmetic and copies ran while one was open for 1% of the time, Pallas kernels for 11%

profile of v4, /device:TPU:1, one launch (start us, length us, event | category | flops | bytes accessed | tf_op | source)
XLA Modules:
  0.0 204.0 jit_solution(8570714881320482124)
XLA Ops:
  7.2 0.0 all-gather.4.cloned.1.call-start
  7.2 2.4 %shard_map.77.grad_ref = bf16[256,1024]{1,0:T(8,128)(2,1)} custom-call(bf16[128,1024]{1,0:T(8,128)(2,1)} %bitcast.18, bf16[128,1024]{1,0:T(8,128)(2,1)} %bitcast.20, bf16[4,1024]{1,0:T(4,128)(2,1)} %bitcast.29, bf16[128,1024]{1,0:T(8,128)(2,1)} %bitcast.26), custom_call_target="tpu_custom_call" | custom-call | tf_op jit(solution)/shard_map/pallas_call | solution.py:71
  9.6 0.0 reduce-scatter.2.cloned.1.call-start
  9.7 0.7 slice_bitcast_fusion
  10.4 1.3 collective-permute-start
  11.7 4.4 %collective-permute-done.next_ref = bf16[16,1024]{1,0:T(8,128)(2,1)S(1)} collective-permute-done((bf16[16,1024]{1,0:T(8,128)(2,1)S(1)}, bf16[16,1024]{1,0:T(8,128)(2,1)S(1)}, u32[]{:S(2)}, u32[]{:S(2)}) %collective-permute-start) | collective-permute-done | bytes 32800 | tf_op jit(solution)/shard_map/ppermute | solution.py:413
  16.1 0.6 copy-done.2
  16.7 2.4 %shard_map.78 = (f32[128,512]{1,0:T(8,128)}, bf16[16,512]{1,0:T(8,128)(2,1)}) custom-call(bf16[128,1024]{1,0:T(8,128)(2,1)} %bitcast.19, bf16[128,1024]{1,0:T(8,128)(2,1)} %bitcast.21, bf16[16,1024]{1,0:T(8,128)(2,1)} %copy-done.2, bf16[4,1024]{1,0:T(4,128)(2,1)} %bitcast.30, bf16[256,1024]{1,0:T(8,128)(2,1)} %shard_map.77.grad_ref, bf16[1024,512]{1,0:T(8,128)(2,1)} %bitcast.23), custom_call_target="tpu_custom_call" | custom-call | tf_op jit(solution)/shard_map/pallas_call | solution.py:103
  19.1 16.8 %all_to_all.15 = f32[8,16,512]{2,1,0:T(8,128)S(1)} all-to-all(f32[8,16,512]{2,1,0:T(8,128)} %bitcast.28), channel_id=1, replica_groups=mesh['pipe'=4,'seq'=16,'tensor'=8] {'tensor'}, dimensions={0} | all-to-all | bytes 524288 | tf_op jit(solution)/shard_map/all_to_all | solution.py:421
  36.0 0.7 pad_maximum_fusion.1
  36.7 35.6 %all-gather.1 = bf16[512,512]{1,0:T(8,128)(2,1)S(1)} all-gather(bf16[32,512]{1,0:T(8,128)(2,1)S(1)} %pad_maximum_fusion.1), channel_id=3, replica_groups=mesh['pipe'=4,'seq'=16,'tensor'=8] {'seq'}, dimensions={0}, use_global_device_ids=true | all-gather | bytes 557056 | tf_op jit(solution)/shard_map/all_gather | solution.py:424
  72.3 0.7 fusion
  73.0 0.3 broadcast_in_dim.12
  73.3 35.0 %all_to_all.16.rows_ref = bf16[8,16,16,512]{3,2,1,0:T(8,128)(2,1)} all-to-all(bf16[8,16,16,512]{3,2,1,0:T(8,128)(2,1)S(1)} %broadcast_in_dim.12), channel_id=1, replica_groups=mesh['pipe'=4,'seq'=16,'tensor'=8] {'tensor'}, dimensions={0} | all-to-all | bytes 4194304 | tf_op jit(solution)/shard_map/all_to_all | solution.py:426
  108.3 19.3 %all-gather.4.cloned.1.call-done = bf16[4096,1024]{1,0:T(8,128)(2,1)} async-done(((bf16[256,1024]{1,0:T(8,128)(2,1)}), bf16[4096,1024]{1,0:T(8,128)(2,1)}) %all-gather.4.cloned.1.call-update) | async-done | bytes 8388624 | tf_op jit(solution)/shard_map/all_gather | solution.py:419
  127.5 13.0 %shard_map.79 = (f32[1024,512]{1,0:T(8,128)}, f32[1280,128]{1,0:T(8,128)}, bf16[2048,512]{1,0:T(8,128)(2,1)}) custom-call(bf16[16,256,1024]{2,1,0:T(8,128)(2,1)} %bitcast.16, bf16[8,16,16,512]{3,2,1,0:T(8,128)(2,1)} %all_to_all.16.rows_ref, bf16[16,16,512]{2,1,0:T(8,128)(2,1)} %get-tuple-element.16.edge_ref, bf16[512,1024]{1,0:T(8,128)(2,1)} %bitcast.22), custom_call_target="tpu_custom_call" | custom-call | tf_op jit(solution)/shard_map/pallas_call | solution.py:216
  140.6 1.1 copy-done.1
  141.7 15.8 %all_to_all.17 = f32[8,160,128]{2,1,0:T(8,128)S(1)} all-to-all(f32[8,160,128]{2,1,0:T(8,128)S(1)} %bitcast.25), channel_id=1, replica_groups=mesh['pipe'=4,'seq'=16,'tensor'=8] {'tensor'}, dimensions={0} | all-to-all | bytes 1310720 | tf_op jit(solution)/shard_map/all_to_all | solution.py:432
  157.5 14.6 %all_gather.19.gram_ref = f32[1280,128]{1,0:T(8,128)S(1)} all-gather(f32[160,128]{1,0:T(8,128)S(1)} %reduce_sum.19), channel_id=1, replica_groups=mesh['pipe'=4,'seq'=16,'tensor'=8] {'tensor'}, dimensions={0}, use_global_device_ids=true | all-gather | bytes 737280 | tf_op jit(solution)/shard_map/all_gather | solution.py:433
  172.1 13.5 %shard_map.80.part_ref = f32[512,512]{1,0:T(8,128)S(1)} custom-call(f32[1280,128]{1,0:T(8,128)S(1)} %all_gather.19.gram_ref), custom_call_target="tpu_custom_call" | custom-call | tf_op jit(solution)/shard_map/pallas_call | solution.py:381
  185.6 0.0 reduce-scatter.2.cloned.1.call-done
  185.6 3.9 %collective-permute-start.1 = (bf16[256,512]{1,0:T(8,128)(2,1)}, bf16[256,512]{1,0:T(8,128)(2,1)S(1)}, u32[]{:S(2)}, u32[]{:S(2)}) collective-permute-start(bf16[256,512]{1,0:T(8,128)(2,1)} %reduce-scatter.2.cloned.1.call-done), channel_id=1, source_target_pairs={{0,384},{128,0},{256,128},{384,256},{1,385},{129,1},{257,129},{385... | collective-permute-start | bytes 786440 | tf_op jit(solution)/shard_map/ppermute | solution.py:436
  189.6 6.9 %shard_map.81 = bf16[1024,512]{1,0:T(8,128)(2,1)} custom-call(f32[512,512]{1,0:T(8,128)S(1)} %shard_map.80.part_ref, f32[1024,512]{1,0:T(8,128)S(1)} %copy-done), custom_call_target="tpu_custom_call" | custom-call | tf_op jit(solution)/shard_map/pallas_call | solution.py:393
  196.5 0.7 copy.9
  (10 shorter events, 0.1 us)
Async XLA Ops:
  7.2 120.4 %all-gather.4.cloned.1.call-start = ((), (), s32[]{:S(2)}) async-start(), calls=%async_computation.5 | async-start | bytes 8912896 | tf_op jit(solution)/shard_map/all_gather | solution.py:419
  9.6 176.0 %reduce-scatter.2.cloned.1.call-start = ((), (), s32[]{:S(2)}) async-start(), calls=%async_computation.4 | async-start | bytes 2359296 | tf_op jit(solution)/shard_map/reduce_scatter | solution.py:431
  10.4 5.7 %collective-permute-start = (bf16[16,1024]{1,0:T(8,128)(2,1)S(1)}, bf16[16,1024]{1,0:T(8,128)(2,1)S(1)}, u32[]{:S(2)}, u32[]{:S(2)}) collective-permute-start(bf16[16,1024]{1,0:T(8,128)(2,1)S(1)} %pad_maximum_fusion), channel_id=1, source_target_pairs={{8,0},{16,8},{24,16},{32,24},{40,32},{48,40},{56,48},{64,56},{72,6... | collective-permute-start | bytes 98312 | tf_op jit(solution)/shard_map/ppermute | solution.py:413
  16.1 0.6 copy-start.2
  140.6 1.1 copy-start.1
  141.7 47.9 %copy-start = (f32[1024,512]{1,0:T(8,128)S(1)}, f32[1024,512]{1,0:T(8,128)}, u32[]{:S(2)}) copy-start(f32[1024,512]{1,0:T(8,128)} %get-tuple-element.21.sketch_ref) | copy-start | bytes 6291460
  185.6 10.9 %collective-permute-start.1 = (bf16[256,512]{1,0:T(8,128)(2,1)}, bf16[256,512]{1,0:T(8,128)(2,1)S(1)}, u32[]{:S(2)}, u32[]{:S(2)}) collective-permute-start(bf16[256,512]{1,0:T(8,128)(2,1)} %reduce-scatter.2.cloned.1.call-done), channel_id=1, source_target_pairs={{0,384},{128,0},{256,128},{384,256},{1,385},{129,1},{257,129},{385... | collective-permute-start | bytes 786440 | tf_op jit(solution)/shard_map/ppermute | solution.py:436
Sparse Core Ops, SparseCore 0:
  10.7 116.8 all-gather.3
  140.8 38.6 reduce-scatter.1

commit v5 on v4

--- a/solution.py
+++ b/solution.py
@@ -84,9 +84,12 @@
     after = next_ref[...].astype(F)
     held[EDGE : EDGE + 8, :] = pre_grad(after[0:8, :], after[8:16, :])
     edge = convolved(held, taps_ref[...].astype(F), EDGE)
-    half = edge.shape[1] // 2
-    wide = edge.astype(F)
-    edge_ref[...] = jnp.concatenate([wide[8:EDGE, half:], wide[8:EDGE, 0:half]], axis=0).astype(B)
+    quarter = edge.shape[1] // 4
+    upper = lax.broadcasted_iota(jnp.int32, (8, quarter), 0) < 4
+    last = edge.astype(F)[8:EDGE, :]
+    last = [last[:, q * quarter : (q + 1) * quarter] for q in range(4)]
+    pairs = [jnp.where(upper, pltpu.roll(last[q], 4, 0), last[q + 1]) for q in (0, 2)]
+    edge_ref[...] = jnp.concatenate(pairs, axis=0).astype(B)
     rows = grad_ref.shape[0]
     grad = jnp.concatenate([grad_ref[0 : rows - EDGE, :], edge], axis=0)
     rows_ref[...] = jnp.dot(grad, test_ref[...], preferred_element_type=F)
@@ -105,7 +108,7 @@
         grid=(1,),
         out_shape=(
             jax.ShapeDtypeStruct((rows, rank), F),
-            jax.ShapeDtypeStruct((EDGE, width // 2), B),
+            jax.ShapeDtypeStruct((EDGE, width // 4), B),
         ),
         in_specs=[
             pl.BlockSpec((EDGE, width), lambda i: (last, 0)),
@@ -115,7 +118,7 @@
             pl.BlockSpec((rows, width), lambda i: (1, 0)),
             whole(*test.shape),
         ],
-        out_specs=(whole(rows, rank), whole(EDGE, width // 2)),
+        out_specs=(whole(rows, rank), whole(EDGE, width // 4)),
         scratch_shapes=[pltpu.VMEM((EDGE + 8, width), F)],
         compiler_params=pltpu.CompilerParams(vmem_limit_bytes=WIDE),
     )(conv, act, after, taps, both, test)
@@ -183,17 +186,21 @@
                     gram[at : at + 128, :] += piece
                 at += 128
     gram_copy.start()
-    half = width // 2
-    final = lax.broadcasted_iota(jnp.int32, (EDGE, half), 0) >= 8
+    quarter = width // 4
+    final = lax.broadcasted_iota(jnp.int32, (8, quarter), 0) >= 4
     weight_copy.wait()
     for i in range(chunks):
         grads_copy(i).wait()
         for z in range(each):
             edge = edge_ref[i * each + z].astype(F)
-            other = jnp.concatenate([edge[8:EDGE, :], edge[0:8, :]], axis=0)
             old = grads[i, z, tokens - EDGE : tokens, :].astype(F)
-            new = [jnp.where(final, edge, old[:, 0:half]), jnp.where(final, other, old[:, half:])]
-            grads[i, z, tokens - EDGE : tokens, :] = jnp.concatenate(new, axis=1).astype(B)
+            new = []
+            for q in range(4):
+                rows = edge[8 * (q // 2) : 8 * (q // 2) + 8, :]
+                rows = rows if q % 2 else pltpu.roll(rows, 4, 0)
+                new.append(jnp.where(final, rows, old[8:EDGE, q * quarter : (q + 1) * quarter]))
+            new = jnp.concatenate([old[0:8, :], jnp.concatenate(new, axis=1)], axis=0)
+            grads[i, z, tokens - EDGE : tokens, :] = new.astype(B)
         left = grads[i].reshape(each * tokens, width)
         terms[i] = dot(left, weights[...], 1, 1, None).astype(B)
         terms_copy(i).start()
@@ -420,9 +427,8 @@
     row_terms, edge = edge_and_rows(conv, act, after, taps, both, sketch_matrix[0])
     row_terms = lax.all_to_all(row_terms.reshape(groups, -1, rank), "tensor", 0, 0, tiled=True)
     rows = jnp.sum(row_terms, axis=0).astype(B)
-    share = rows.shape[0]
-    small = lax.all_gather(jnp.concatenate([rows, edge], axis=0), "seq", axis=0)
-    rows, edges = small[:, :share], small[:, share:]
+    small = lax.all_gather(jnp.concatenate([rows, edge], axis=1), "seq", axis=0)
+    rows, edges = small[:, :, :rank], small[:, :, rank:]
     rows = lax.all_to_all(
         jnp.broadcast_to(rows[None], (groups,) + rows.shape), "tensor", 0, 0, tiled=True
     )

time: 205 us -> 203 us (level)
  blocking collectives: 118 us -> 80.1 us
  waiting for transfers between devices: 23.7 us -> 49.6 us
  starting transfers between devices: 5.25 us -> 14.3 us
    all_to_all x1 -> x0, blocking collectives: 35 us -> none  [local(): lax.all_to_all(jnp.broadcast_to(rows[None], (groups,) + rows.shape), 'ten...]
    all_to_all x0 -> x1, waiting for transfers between devices: none -> 25.7 us  [local(): lax.all_to_all(jnp.broadcast_to(rows[None], (groups,) + rows.shape), 'ten...]
    all_to_all x0 -> x1, starting transfers between devices: none -> 9.02 us  [local(): lax.all_to_all(jnp.broadcast_to(rows[None], (groups,) + rows.shape), 'ten...]
    all_gather x1, blocking collectives: 35.6 us -> 33 us  [local(): small = lax.all_gather(jnp.concatenate([rows, edge], axis=1), 'seq', axis=0)]
  transfers between devices with their start and end apart: 4 -> 5, of which waited for: 2 -> 3; matrix products, arithmetic and copies ran while one was open for 1% -> 2% of each run, Pallas kernels for 11% -> 11%
where the time goes in v5:
time: 203 us
  blocking collectives  80.1 us (39%)
  waiting for transfers between devices  49.6 us (24%)
  Pallas kernels  38.3 us (19%)
  starting transfers between devices  14.3 us (7%)
  between operations  14.1 us (7%)
  local copies, waits for them, and re-layouts  5.43 us (3%)
    all_gather x1, blocking collectives, local(): small = lax.all_gather(jnp.concatenate([rows, edge], axis=1), 'seq', axis=0)  33 us
    all_to_all x1, waiting for transfers between devices, local(): lax.all_to_all(jnp.broadcast_to(rows[None], (groups,) + rows.shape), 'ten...  25.7 us
    all_gather x1, waiting for transfers between devices, local(): gathered = lax.all_gather(both, 'seq', axis=0)  19.5 us
    all_to_all x1, blocking collectives, local(): lax.all_to_all(row_terms.reshape(groups, -1, rank), 'tensor', 0, 0, tiled...  16.8 us
    all_to_all x1, blocking collectives, local(): lax.all_to_all(gram.reshape(groups, -1, 128), 'tensor', 0, 0, tiled=True)  15.8 us
    all_gather x1, blocking collectives, local(): gram = lax.all_gather(jnp.sum(gram, axis=0), 'tensor', axis=0, tiled=True)  14.5 us
    pallas_call x1, Pallas kernels, factored(): pl.pallas_call(functools.partial(factor_kernel, blocks, FIRST), out_shape...  13.5 us
    pallas_call x1, Pallas kernels, middle(): pl.pallas_call(middle_kernel, out_shape=(jax.ShapeDtypeStruct((width, ran...  13 us
  transfers between devices with their start and end apart: 5, of which 3 were waited for; matrix products, arithmetic and copies ran while one was open for 2% of the time, Pallas kernels for 11%

profile of v5, /device:TPU:1, one launch (start us, length us, event | category | flops | bytes accessed | tf_op | source)
XLA Modules:
  0.0 202.6 jit_solution(17649121803365213082)
XLA Ops:
  7.2 0.0 all-gather.4.cloned.1.call-start
  7.2 2.4 %shard_map.77.grad_ref = bf16[256,1024]{1,0:T(8,128)(2,1)} custom-call(bf16[128,1024]{1,0:T(8,128)(2,1)} %bitcast.19, bf16[128,1024]{1,0:T(8,128)(2,1)} %bitcast.21, bf16[4,1024]{1,0:T(4,128)(2,1)} %bitcast.30, bf16[128,1024]{1,0:T(8,128)(2,1)} %bitcast.27), custom_call_target="tpu_custom_call" | custom-call | tf_op jit(solution)/shard_map/pallas_call | solution.py:71
  9.6 0.7 slice_bitcast_fusion
  10.4 1.3 collective-permute-start
  11.7 4.4 %collective-permute-done.next_ref = bf16[16,1024]{1,0:T(8,128)(2,1)S(1)} collective-permute-done((bf16[16,1024]{1,0:T(8,128)(2,1)S(1)}, bf16[16,1024]{1,0:T(8,128)(2,1)S(1)}, u32[]{:S(2)}, u32[]{:S(2)}) %collective-permute-start) | collective-permute-done | bytes 32800 | tf_op jit(solution)/shard_map/ppermute | solution.py:420
  16.0 0.6 copy-done.3
  16.6 2.4 %shard_map.78 = (f32[128,512]{1,0:T(8,128)}, bf16[16,256]{1,0:T(8,128)(2,1)}) custom-call(bf16[128,1024]{1,0:T(8,128)(2,1)} %bitcast.20, bf16[128,1024]{1,0:T(8,128)(2,1)} %bitcast.22, bf16[16,1024]{1,0:T(8,128)(2,1)} %copy-done.3, bf16[4,1024]{1,0:T(4,128)(2,1)} %bitcast.31, bf16[256,1024]{1,0:T(8,128)(2,1)} %shard_map.77.grad_ref, bf16[1024,512]{1,0:T(8,128)(2,1)} %bitcast.24), custom_call_target="tpu_custom_call" | custom-call | tf_op jit(solution)/shard_map/pallas_call | solution.py:106
  19.1 16.8 %all_to_all.15 = f32[8,16,512]{2,1,0:T(8,128)S(1)} all-to-all(f32[8,16,512]{2,1,0:T(8,128)} %bitcast.29), channel_id=1, replica_groups=mesh['pipe'=4,'seq'=16,'tensor'=8] {'tensor'}, dimensions={0} | all-to-all | bytes 524288 | tf_op jit(solution)/shard_map/all_to_all | solution.py:428
  35.9 0.7 pad_maximum_fusion.1
  36.6 33.0 %all-gather.1 = bf16[256,768]{1,0:T(8,128)(2,1)S(1)} all-gather(bf16[16,768]{1,0:T(8,128)(2,1)S(1)} %pad_maximum_fusion.1), channel_id=3, replica_groups=mesh['pipe'=4,'seq'=16,'tensor'=8] {'seq'}, dimensions={0}, use_global_device_ids=true | all-gather | bytes 417792 | tf_op jit(solution)/shard_map/all_gather | solution.py:430
  69.6 1.6 broadcast_in_dim.12
  71.2 9.0 %all-to-all-start.1 = ((bf16[8,16,16,512]{3,2,1,0:T(8,128)(2,1)}), bf16[8,16,16,512]{3,2,1,0:T(8,128)(2,1)S(1)}, u32[]{:S(2)}, u32[]{:S(2)}) async-start(bf16[8,16,16,512]{3,2,1,0:T(8,128)(2,1)} %broadcast_in_dim.12), calls=%async_computation.1 | async-start | bytes 4194304 | tf_op jit(solution)/shard_map/all_to_all | solution.py:432
  80.3 0.7 slice.25.edge_ref
  80.9 25.7 %all-to-all-done.1.rows_ref = bf16[8,16,16,512]{3,2,1,0:T(8,128)(2,1)S(1)} async-done(((bf16[8,16,16,512]{3,2,1,0:T(8,128)(2,1)}), bf16[8,16,16,512]{3,2,1,0:T(8,128)(2,1)S(1)}, u32[]{:S(2)}, u32[]{:S(2)}) %all-to-all-start.1) | async-done | bytes 2097184 | tf_op jit(solution)/shard_map/all_to_all | solution.py:432
  106.6 19.5 %all-gather.4.cloned.1.call-done = bf16[4096,1024]{1,0:T(8,128)(2,1)} async-done(((bf16[256,1024]{1,0:T(8,128)(2,1)}), bf16[4096,1024]{1,0:T(8,128)(2,1)}) %all-gather.4.cloned.1.call-update) | async-done | bytes 8388624 | tf_op jit(solution)/shard_map/all_gather | solution.py:426
  126.1 13.0 %shard_map.79 = (f32[1024,512]{1,0:T(8,128)}, f32[1280,128]{1,0:T(8,128)}, bf16[2048,512]{1,0:T(8,128)(2,1)}) custom-call(bf16[16,256,1024]{2,1,0:T(8,128)(2,1)} %bitcast.16, bf16[8,16,16,512]{3,2,1,0:T(8,128)(2,1)} %copy-done.1, bf16[16,16,256]{2,1,0:T(8,128)(2,1)} %slice.25.edge_ref, bf16[512,1024]{1,0:T(8,128)(2,1)} %bitcast.23), custom_call_target="tpu_custom_call" | custom-call | tf_op jit(solution)/shard_map/pallas_call | solution.py:223
  139.2 1.1 copy-done.2
  140.3 15.8 %all_to_all.16 = f32[8,160,128]{2,1,0:T(8,128)S(1)} all-to-all(f32[8,160,128]{2,1,0:T(8,128)S(1)} %bitcast.26), channel_id=1, replica_groups=mesh['pipe'=4,'seq'=16,'tensor'=8] {'tensor'}, dimensions={0} | all-to-all | bytes 1310720 | tf_op jit(solution)/shard_map/all_to_all | solution.py:438
  156.1 14.5 %all_gather.19.gram_ref = f32[1280,128]{1,0:T(8,128)S(1)} all-gather(f32[160,128]{1,0:T(8,128)S(1)} %reduce_sum.19), channel_id=1, replica_groups=mesh['pipe'=4,'seq'=16,'tensor'=8] {'tensor'}, dimensions={0}, use_global_device_ids=true | all-gather | bytes 737280 | tf_op jit(solution)/shard_map/all_gather | solution.py:439
  170.6 13.5 %shard_map.80.part_ref = f32[512,512]{1,0:T(8,128)S(1)} custom-call(f32[1280,128]{1,0:T(8,128)S(1)} %all_gather.19.gram_ref), custom_call_target="tpu_custom_call" | custom-call | tf_op jit(solution)/shard_map/pallas_call | solution.py:388
  184.1 0.0 reduce-scatter.2.cloned.1.call-done
  184.2 4.0 %collective-permute-start.1 = (bf16[256,512]{1,0:T(8,128)(2,1)}, bf16[256,512]{1,0:T(8,128)(2,1)S(1)}, u32[]{:S(2)}, u32[]{:S(2)}) collective-permute-start(bf16[256,512]{1,0:T(8,128)(2,1)} %reduce-scatter.2.cloned.1.call-done), channel_id=1, source_target_pairs={{0,384},{128,0},{256,128},{384,256},{1,385},{129,1},{257,129},{385... | collective-permute-start | bytes 786440 | tf_op jit(solution)/shard_map/ppermute | solution.py:442
  188.1 6.9 %shard_map.81 = bf16[1024,512]{1,0:T(8,128)(2,1)} custom-call(f32[512,512]{1,0:T(8,128)S(1)} %shard_map.80.part_ref, f32[1024,512]{1,0:T(8,128)S(1)} %copy-done), custom_call_target="tpu_custom_call" | custom-call | tf_op jit(solution)/shard_map/pallas_call | solution.py:400
  195.1 0.7 copy.9
  (14 shorter events, 0.1 us)
Async XLA Ops:
  7.2 119.0 %all-gather.4.cloned.1.call-start = ((), (), s32[]{:S(2)}) async-start(), calls=%async_computation.5 | async-start | bytes 8912896 | tf_op jit(solution)/shard_map/all_gather | solution.py:426
  10.4 5.7 %collective-permute-start = (bf16[16,1024]{1,0:T(8,128)(2,1)S(1)}, bf16[16,1024]{1,0:T(8,128)(2,1)S(1)}, u32[]{:S(2)}, u32[]{:S(2)}) collective-permute-start(bf16[16,1024]{1,0:T(8,128)(2,1)S(1)} %pad_maximum_fusion), channel_id=1, source_target_pairs={{8,0},{16,8},{24,16},{32,24},{40,32},{48,40},{56,48},{64,56},{72,6... | collective-permute-start | bytes 98312 | tf_op jit(solution)/shard_map/ppermute | solution.py:420
  16.0 0.6 copy-start.3
  71.2 35.4 %all-to-all-start.1 = ((bf16[8,16,16,512]{3,2,1,0:T(8,128)(2,1)}), bf16[8,16,16,512]{3,2,1,0:T(8,128)(2,1)S(1)}, u32[]{:S(2)}, u32[]{:S(2)}) async-start(bf16[8,16,16,512]{3,2,1,0:T(8,128)(2,1)} %broadcast_in_dim.12), calls=%async_computation.1 | async-start | bytes 4194304 | tf_op jit(solution)/shard_map/all_to_all | solution.py:432
  80.3 103.9 %reduce-scatter.2.cloned.1.call-start = ((), (), s32[]{:S(2)}) async-start(), calls=%async_computation.4 | async-start | bytes 2359296 | tf_op jit(solution)/shard_map/reduce_scatter | solution.py:437
  106.6 19.5 %copy-start.1 = (bf16[8,16,16,512]{3,2,1,0:T(8,128)(2,1)}, bf16[8,16,16,512]{3,2,1,0:T(8,128)(2,1)S(1)}, u32[]{:S(2)}) copy-start(bf16[8,16,16,512]{3,2,1,0:T(8,128)(2,1)S(1)} %all-to-all-done.1.rows_ref) | copy-start | bytes 6291460
  139.2 1.1 copy-start.2
  140.3 47.9 %copy-start = (f32[1024,512]{1,0:T(8,128)S(1)}, f32[1024,512]{1,0:T(8,128)}, u32[]{:S(2)}) copy-start(f32[1024,512]{1,0:T(8,128)} %get-tuple-element.21.sketch_ref) | copy-start | bytes 6291460
  184.2 10.9 %collective-permute-start.1 = (bf16[256,512]{1,0:T(8,128)(2,1)}, bf16[256,512]{1,0:T(8,128)(2,1)S(1)}, u32[]{:S(2)}, u32[]{:S(2)}) collective-permute-start(bf16[256,512]{1,0:T(8,128)(2,1)} %reduce-scatter.2.cloned.1.call-done), channel_id=1, source_target_pairs={{0,384},{128,0},{256,128},{384,256},{1,385},{129,1},{257,129},{385... | collective-permute-start | bytes 786440 | tf_op jit(solution)/shard_map/ppermute | solution.py:442
Sparse Core Ops, SparseCore 0:
  10.7 115.4 all-gather.3
  139.3 38.6 reduce-scatter.1

commit v6 on v5

--- a/solution.py
+++ b/solution.py
@@ -218,7 +218,7 @@
     blocks = rank // 128
     packed = blocks * (blocks + 1) // 2 * 128
     outs = weights.shape[0]
-    chunks = 4
+    chunks = 2
     each = shards // chunks
     return pl.pallas_call(
         middle_kernel,

time: 203 us -> 203 us (level)
  no operation moved by 1% of the time
where the time goes in v6:
time: 203 us; the launch traced here: 202 us
  blocking collectives  80.1 us (39%)
  waiting for transfers between devices  49.6 us (24%)
  Pallas kernels  37.6 us (19%)
  starting transfers between devices  14.3 us (7%)
  between operations  14.1 us (7%)
  local copies, waits for them, and re-layouts  5.43 us (3%)
    all_gather x1, blocking collectives, local(): small = lax.all_gather(jnp.concatenate([rows, edge], axis=1), 'seq', axis=0)  33 us
    all_to_all x1, waiting for transfers between devices, local(): lax.all_to_all(jnp.broadcast_to(rows[None], (groups,) + rows.shape), 'ten...  25.7 us
    all_gather x1, waiting for transfers between devices, local(): gathered = lax.all_gather(both, 'seq', axis=0)  19.5 us
    all_to_all x1, blocking collectives, local(): lax.all_to_all(row_terms.reshape(groups, -1, rank), 'tensor', 0, 0, tiled...  16.8 us
    all_to_all x1, blocking collectives, local(): lax.all_to_all(gram.reshape(groups, -1, 128), 'tensor', 0, 0, tiled=True)  15.8 us
    all_gather x1, blocking collectives, local(): gram = lax.all_gather(jnp.sum(gram, axis=0), 'tensor', axis=0, tiled=True)  14.6 us
    pallas_call x1, Pallas kernels, factored(): pl.pallas_call(functools.partial(factor_kernel, blocks, FIRST), out_shape...  13.5 us
    pallas_call x1, Pallas kernels, middle(): pl.pallas_call(middle_kernel, out_shape=(jax.ShapeDtypeStruct((width, ran...  12.4 us
  transfers between devices with their start and end apart: 5, of which 3 were waited for; matrix products, arithmetic and copies ran while one was open for 2% of the time, Pallas kernels for 11%

profile of v6, /device:TPU:1, one launch (start us, length us, event | category | flops | bytes accessed | tf_op | source)
XLA Modules:
  0.0 202.0 jit_solution(4418897004384203620)
XLA Ops:
  7.2 0.0 all-gather.4.cloned.1.call-start
  7.2 2.4 %shard_map.77.grad_ref = bf16[256,1024]{1,0:T(8,128)(2,1)} custom-call(bf16[128,1024]{1,0:T(8,128)(2,1)} %bitcast.19, bf16[128,1024]{1,0:T(8,128)(2,1)} %bitcast.21, bf16[4,1024]{1,0:T(4,128)(2,1)} %bitcast.30, bf16[128,1024]{1,0:T(8,128)(2,1)} %bitcast.27), custom_call_target="tpu_custom_call" | custom-call | tf_op jit(solution)/shard_map/pallas_call | solution.py:71
  9.6 0.7 slice_bitcast_fusion
  10.4 1.3 collective-permute-start
  11.7 4.4 %collective-permute-done.next_ref = bf16[16,1024]{1,0:T(8,128)(2,1)S(1)} collective-permute-done((bf16[16,1024]{1,0:T(8,128)(2,1)S(1)}, bf16[16,1024]{1,0:T(8,128)(2,1)S(1)}, u32[]{:S(2)}, u32[]{:S(2)}) %collective-permute-start) | collective-permute-done | bytes 32800 | tf_op jit(solution)/shard_map/ppermute | solution.py:420
  16.0 0.6 copy-done.3
  16.6 2.4 %shard_map.78 = (f32[128,512]{1,0:T(8,128)}, bf16[16,256]{1,0:T(8,128)(2,1)}) custom-call(bf16[128,1024]{1,0:T(8,128)(2,1)} %bitcast.20, bf16[128,1024]{1,0:T(8,128)(2,1)} %bitcast.22, bf16[16,1024]{1,0:T(8,128)(2,1)} %copy-done.3, bf16[4,1024]{1,0:T(4,128)(2,1)} %bitcast.31, bf16[256,1024]{1,0:T(8,128)(2,1)} %shard_map.77.grad_ref, bf16[1024,512]{1,0:T(8,128)(2,1)} %bitcast.24), custom_call_target="tpu_custom_call" | custom-call | tf_op jit(solution)/shard_map/pallas_call | solution.py:106
  19.1 16.8 %all_to_all.15 = f32[8,16,512]{2,1,0:T(8,128)S(1)} all-to-all(f32[8,16,512]{2,1,0:T(8,128)} %bitcast.29), channel_id=1, replica_groups=mesh['pipe'=4,'seq'=16,'tensor'=8] {'tensor'}, dimensions={0} | all-to-all | bytes 524288 | tf_op jit(solution)/shard_map/all_to_all | solution.py:428
  35.9 0.7 pad_maximum_fusion.1
  36.6 33.0 %all-gather.1 = bf16[256,768]{1,0:T(8,128)(2,1)S(1)} all-gather(bf16[16,768]{1,0:T(8,128)(2,1)S(1)} %pad_maximum_fusion.1), channel_id=3, replica_groups=mesh['pipe'=4,'seq'=16,'tensor'=8] {'seq'}, dimensions={0}, use_global_device_ids=true | all-gather | bytes 417792 | tf_op jit(solution)/shard_map/all_gather | solution.py:430
  69.6 1.6 broadcast_in_dim.12
  71.2 9.0 %all-to-all-start.1 = ((bf16[8,16,16,512]{3,2,1,0:T(8,128)(2,1)}), bf16[8,16,16,512]{3,2,1,0:T(8,128)(2,1)S(1)}, u32[]{:S(2)}, u32[]{:S(2)}) async-start(bf16[8,16,16,512]{3,2,1,0:T(8,128)(2,1)} %broadcast_in_dim.12), calls=%async_computation.1 | async-start | bytes 4194304 | tf_op jit(solution)/shard_map/all_to_all | solution.py:432
  80.3 0.7 slice.25.edge_ref
  80.9 25.7 %all-to-all-done.1.rows_ref = bf16[8,16,16,512]{3,2,1,0:T(8,128)(2,1)S(1)} async-done(((bf16[8,16,16,512]{3,2,1,0:T(8,128)(2,1)}), bf16[8,16,16,512]{3,2,1,0:T(8,128)(2,1)S(1)}, u32[]{:S(2)}, u32[]{:S(2)}) %all-to-all-start.1) | async-done | bytes 2097184 | tf_op jit(solution)/shard_map/all_to_all | solution.py:432
  106.6 19.5 %all-gather.4.cloned.1.call-done = bf16[4096,1024]{1,0:T(8,128)(2,1)} async-done(((bf16[256,1024]{1,0:T(8,128)(2,1)}), bf16[4096,1024]{1,0:T(8,128)(2,1)}) %all-gather.4.cloned.1.call-update) | async-done | bytes 8388624 | tf_op jit(solution)/shard_map/all_gather | solution.py:426
  126.1 12.4 %shard_map.79 = (f32[1024,512]{1,0:T(8,128)}, f32[1280,128]{1,0:T(8,128)}, bf16[2048,512]{1,0:T(8,128)(2,1)}) custom-call(bf16[16,256,1024]{2,1,0:T(8,128)(2,1)} %bitcast.16, bf16[8,16,16,512]{3,2,1,0:T(8,128)(2,1)} %copy-done.1, bf16[16,16,256]{2,1,0:T(8,128)(2,1)} %slice.25.edge_ref, bf16[512,1024]{1,0:T(8,128)(2,1)} %bitcast.23), custom_call_target="tpu_custom_call" | custom-call | tf_op jit(solution)/shard_map/pallas_call | solution.py:223
  138.6 1.1 copy-done.2
  139.6 15.8 %all_to_all.16 = f32[8,160,128]{2,1,0:T(8,128)S(1)} all-to-all(f32[8,160,128]{2,1,0:T(8,128)S(1)} %bitcast.26), channel_id=1, replica_groups=mesh['pipe'=4,'seq'=16,'tensor'=8] {'tensor'}, dimensions={0} | all-to-all | bytes 1310720 | tf_op jit(solution)/shard_map/all_to_all | solution.py:438
  155.5 14.6 %all_gather.19.gram_ref = f32[1280,128]{1,0:T(8,128)S(1)} all-gather(f32[160,128]{1,0:T(8,128)S(1)} %reduce_sum.19), channel_id=1, replica_groups=mesh['pipe'=4,'seq'=16,'tensor'=8] {'tensor'}, dimensions={0}, use_global_device_ids=true | all-gather | bytes 737280 | tf_op jit(solution)/shard_map/all_gather | solution.py:439
  170.0 13.5 %shard_map.80.part_ref = f32[512,512]{1,0:T(8,128)S(1)} custom-call(f32[1280,128]{1,0:T(8,128)S(1)} %all_gather.19.gram_ref), custom_call_target="tpu_custom_call" | custom-call | tf_op jit(solution)/shard_map/pallas_call | solution.py:388
  183.5 0.0 reduce-scatter.2.cloned.1.call-done
  183.6 3.9 %collective-permute-start.1 = (bf16[256,512]{1,0:T(8,128)(2,1)}, bf16[256,512]{1,0:T(8,128)(2,1)S(1)}, u32[]{:S(2)}, u32[]{:S(2)}) collective-permute-start(bf16[256,512]{1,0:T(8,128)(2,1)} %reduce-scatter.2.cloned.1.call-done), channel_id=1, source_target_pairs={{0,384},{128,0},{256,128},{384,256},{1,385},{129,1},{257,129},{385... | collective-permute-start | bytes 786440 | tf_op jit(solution)/shard_map/ppermute | solution.py:442
  187.5 6.9 %shard_map.81 = bf16[1024,512]{1,0:T(8,128)(2,1)} custom-call(f32[512,512]{1,0:T(8,128)S(1)} %shard_map.80.part_ref, f32[1024,512]{1,0:T(8,128)S(1)} %copy-done), custom_call_target="tpu_custom_call" | custom-call | tf_op jit(solution)/shard_map/pallas_call | solution.py:400
  194.5 0.7 copy.9
  (14 shorter events, 0.1 us)
Async XLA Ops:
  7.2 119.0 %all-gather.4.cloned.1.call-start = ((), (), s32[]{:S(2)}) async-start(), calls=%async_computation.5 | async-start | bytes 8912896 | tf_op jit(solution)/shard_map/all_gather | solution.py:426
  10.4 5.7 %collective-permute-start = (bf16[16,1024]{1,0:T(8,128)(2,1)S(1)}, bf16[16,1024]{1,0:T(8,128)(2,1)S(1)}, u32[]{:S(2)}, u32[]{:S(2)}) collective-permute-start(bf16[16,1024]{1,0:T(8,128)(2,1)S(1)} %pad_maximum_fusion), channel_id=1, source_target_pairs={{8,0},{16,8},{24,16},{32,24},{40,32},{48,40},{56,48},{64,56},{72,6... | collective-permute-start | bytes 98312 | tf_op jit(solution)/shard_map/ppermute | solution.py:420
  16.0 0.6 copy-start.3
  71.2 35.4 %all-to-all-start.1 = ((bf16[8,16,16,512]{3,2,1,0:T(8,128)(2,1)}), bf16[8,16,16,512]{3,2,1,0:T(8,128)(2,1)S(1)}, u32[]{:S(2)}, u32[]{:S(2)}) async-start(bf16[8,16,16,512]{3,2,1,0:T(8,128)(2,1)} %broadcast_in_dim.12), calls=%async_computation.1 | async-start | bytes 4194304 | tf_op jit(solution)/shard_map/all_to_all | solution.py:432
  80.3 103.3 %reduce-scatter.2.cloned.1.call-start = ((), (), s32[]{:S(2)}) async-start(), calls=%async_computation.4 | async-start | bytes 2359296 | tf_op jit(solution)/shard_map/reduce_scatter | solution.py:437
  106.6 19.5 %copy-start.1 = (bf16[8,16,16,512]{3,2,1,0:T(8,128)(2,1)}, bf16[8,16,16,512]{3,2,1,0:T(8,128)(2,1)S(1)}, u32[]{:S(2)}) copy-start(bf16[8,16,16,512]{3,2,1,0:T(8,128)(2,1)S(1)} %all-to-all-done.1.rows_ref) | copy-start | bytes 6291460
  138.6 1.1 copy-start.2
  139.6 47.9 %copy-start = (f32[1024,512]{1,0:T(8,128)S(1)}, f32[1024,512]{1,0:T(8,128)}, u32[]{:S(2)}) copy-start(f32[1024,512]{1,0:T(8,128)} %get-tuple-element.21.sketch_ref) | copy-start | bytes 6291460
  183.6 10.9 %collective-permute-start.1 = (bf16[256,512]{1,0:T(8,128)(2,1)}, bf16[256,512]{1,0:T(8,128)(2,1)S(1)}, u32[]{:S(2)}, u32[]{:S(2)}) collective-permute-start(bf16[256,512]{1,0:T(8,128)(2,1)} %reduce-scatter.2.cloned.1.call-done), channel_id=1, source_target_pairs={{0,384},{128,0},{256,128},{384,256},{1,385},{129,1},{257,129},{385... | collective-permute-start | bytes 786440 | tf_op jit(solution)/shard_map/ppermute | solution.py:442
Sparse Core Ops, SparseCore 0:
  10.7 115.4 all-gather.3
  138.7 38.6 reduce-scatter.1

commit v7 on v6

--- a/solution.py
+++ b/solution.py
@@ -367,17 +367,17 @@
     inv_hi, inv_lo = split(m[...] * scale)
 
     def rows(i, carry):
-        at = pl.multiple_of(i * 256, 256)
-        hi, lo = split(sketch_ref[pl.ds(at, 256), :])
+        at = pl.multiple_of(i * 512, 512)
+        hi, lo = split(sketch_ref[pl.ds(at, 512), :])
         for c in range(0, rank, 256):
             end = min(c + 256, rank)
             left, right = inv_hi[c:end, 0:end], inv_lo[c:end, 0:end]
             out = dot(hi[:, 0:end], left, 1, 1, None)
             out += dot(hi[:, 0:end], right, 1, 1, None) + dot(lo[:, 0:end], left, 1, 1, None)
-            out_ref[pl.ds(at, 256), c:end] = out.astype(B)
+            out_ref[pl.ds(at, 512), c:end] = out.astype(B)
         return carry
 
-    lax.fori_loop(0, sketch_ref.shape[0] // 256, rows, 0)
+    lax.fori_loop(0, sketch_ref.shape[0] // 512, rows, 0)
 
 
 FIRST = 3

time: 203 us -> 202 us (level)
  no operation moved by 1% of the time
where the time goes in v7:
time: 202 us
  blocking collectives  80.1 us (40%)
  waiting for transfers between devices  49.6 us (25%)
  Pallas kernels  37.2 us (18%)
  starting transfers between devices  14.3 us (7%)
  between operations  14.1 us (7%)
  local copies, waits for them, and re-layouts  5.43 us (3%)
    all_gather x1, blocking collectives, local(): small = lax.all_gather(jnp.concatenate([rows, edge], axis=1), 'seq', axis=0)  33 us
    all_to_all x1, waiting for transfers between devices, local(): lax.all_to_all(jnp.broadcast_to(rows[None], (groups,) + rows.shape), 'ten...  25.7 us
    all_gather x1, waiting for transfers between devices, local(): gathered = lax.all_gather(both, 'seq', axis=0)  19.5 us
    all_to_all x1, blocking collectives, local(): lax.all_to_all(row_terms.reshape(groups, -1, rank), 'tensor', 0, 0, tiled...  16.8 us
    all_to_all x1, blocking collectives, local(): lax.all_to_all(gram.reshape(groups, -1, 128), 'tensor', 0, 0, tiled=True)  15.8 us
    all_gather x1, blocking collectives, local(): gram = lax.all_gather(jnp.sum(gram, axis=0), 'tensor', axis=0, tiled=True)  14.6 us
    pallas_call x1, Pallas kernels, factored(): pl.pallas_call(functools.partial(factor_kernel, blocks, FIRST), out_shape...  13.5 us
    pallas_call x1, Pallas kernels, middle(): pl.pallas_call(middle_kernel, out_shape=(jax.ShapeDtypeStruct((width, ran...  12.4 us
  transfers between devices with their start and end apart: 5, of which 3 were waited for; matrix products, arithmetic and copies ran while one was open for 2% of the time, Pallas kernels for 11%

profile of v7, /device:TPU:1, one launch (start us, length us, event | category | flops | bytes accessed | tf_op | source)
XLA Modules:
  0.0 201.6 jit_solution(16614231587135836202)
XLA Ops:
  7.2 0.0 all-gather.4.cloned.1.call-start
  7.2 2.4 %shard_map.77.grad_ref = bf16[256,1024]{1,0:T(8,128)(2,1)} custom-call(bf16[128,1024]{1,0:T(8,128)(2,1)} %bitcast.19, bf16[128,1024]{1,0:T(8,128)(2,1)} %bitcast.21, bf16[4,1024]{1,0:T(4,128)(2,1)} %bitcast.30, bf16[128,1024]{1,0:T(8,128)(2,1)} %bitcast.27), custom_call_target="tpu_custom_call" | custom-call | tf_op jit(solution)/shard_map/pallas_call | solution.py:71
  9.6 0.7 slice_bitcast_fusion
  10.4 1.3 collective-permute-start
  11.7 4.4 %collective-permute-done.next_ref = bf16[16,1024]{1,0:T(8,128)(2,1)S(1)} collective-permute-done((bf16[16,1024]{1,0:T(8,128)(2,1)S(1)}, bf16[16,1024]{1,0:T(8,128)(2,1)S(1)}, u32[]{:S(2)}, u32[]{:S(2)}) %collective-permute-start) | collective-permute-done | bytes 32800 | tf_op jit(solution)/shard_map/ppermute | solution.py:420
  16.0 0.6 copy-done.3
  16.6 2.4 %shard_map.78 = (f32[128,512]{1,0:T(8,128)}, bf16[16,256]{1,0:T(8,128)(2,1)}) custom-call(bf16[128,1024]{1,0:T(8,128)(2,1)} %bitcast.20, bf16[128,1024]{1,0:T(8,128)(2,1)} %bitcast.22, bf16[16,1024]{1,0:T(8,128)(2,1)} %copy-done.3, bf16[4,1024]{1,0:T(4,128)(2,1)} %bitcast.31, bf16[256,1024]{1,0:T(8,128)(2,1)} %shard_map.77.grad_ref, bf16[1024,512]{1,0:T(8,128)(2,1)} %bitcast.24), custom_call_target="tpu_custom_call" | custom-call | tf_op jit(solution)/shard_map/pallas_call | solution.py:106
  19.1 16.8 %all_to_all.15 = f32[8,16,512]{2,1,0:T(8,128)S(1)} all-to-all(f32[8,16,512]{2,1,0:T(8,128)} %bitcast.29), channel_id=1, replica_groups=mesh['pipe'=4,'seq'=16,'tensor'=8] {'tensor'}, dimensions={0} | all-to-all | bytes 524288 | tf_op jit(solution)/shard_map/all_to_all | solution.py:428
  35.9 0.7 pad_maximum_fusion.1
  36.6 33.0 %all-gather.1 = bf16[256,768]{1,0:T(8,128)(2,1)S(1)} all-gather(bf16[16,768]{1,0:T(8,128)(2,1)S(1)} %pad_maximum_fusion.1), channel_id=3, replica_groups=mesh['pipe'=4,'seq'=16,'tensor'=8] {'seq'}, dimensions={0}, use_global_device_ids=true | all-gather | bytes 417792 | tf_op jit(solution)/shard_map/all_gather | solution.py:430
  69.6 1.6 broadcast_in_dim.12
  71.2 9.0 %all-to-all-start.1 = ((bf16[8,16,16,512]{3,2,1,0:T(8,128)(2,1)}), bf16[8,16,16,512]{3,2,1,0:T(8,128)(2,1)S(1)}, u32[]{:S(2)}, u32[]{:S(2)}) async-start(bf16[8,16,16,512]{3,2,1,0:T(8,128)(2,1)} %broadcast_in_dim.12), calls=%async_computation.1 | async-start | bytes 4194304 | tf_op jit(solution)/shard_map/all_to_all | solution.py:432
  80.3 0.7 slice.25.edge_ref
  80.9 25.7 %all-to-all-done.1.rows_ref = bf16[8,16,16,512]{3,2,1,0:T(8,128)(2,1)S(1)} async-done(((bf16[8,16,16,512]{3,2,1,0:T(8,128)(2,1)}), bf16[8,16,16,512]{3,2,1,0:T(8,128)(2,1)S(1)}, u32[]{:S(2)}, u32[]{:S(2)}) %all-to-all-start.1) | async-done | bytes 2097184 | tf_op jit(solution)/shard_map/all_to_all | solution.py:432
  106.6 19.5 %all-gather.4.cloned.1.call-done = bf16[4096,1024]{1,0:T(8,128)(2,1)} async-done(((bf16[256,1024]{1,0:T(8,128)(2,1)}), bf16[4096,1024]{1,0:T(8,128)(2,1)}) %all-gather.4.cloned.1.call-update) | async-done | bytes 8388624 | tf_op jit(solution)/shard_map/all_gather | solution.py:426
  126.1 12.4 %shard_map.79 = (f32[1024,512]{1,0:T(8,128)}, f32[1280,128]{1,0:T(8,128)}, bf16[2048,512]{1,0:T(8,128)(2,1)}) custom-call(bf16[16,256,1024]{2,1,0:T(8,128)(2,1)} %bitcast.16, bf16[8,16,16,512]{3,2,1,0:T(8,128)(2,1)} %copy-done.1, bf16[16,16,256]{2,1,0:T(8,128)(2,1)} %slice.25.edge_ref, bf16[512,1024]{1,0:T(8,128)(2,1)} %bitcast.23), custom_call_target="tpu_custom_call" | custom-call | tf_op jit(solution)/shard_map/pallas_call | solution.py:223
  138.6 1.1 copy-done.2
  139.6 15.8 %all_to_all.16 = f32[8,160,128]{2,1,0:T(8,128)S(1)} all-to-all(f32[8,160,128]{2,1,0:T(8,128)S(1)} %bitcast.26), channel_id=1, replica_groups=mesh['pipe'=4,'seq'=16,'tensor'=8] {'tensor'}, dimensions={0} | all-to-all | bytes 1310720 | tf_op jit(solution)/shard_map/all_to_all | solution.py:438
  155.5 14.6 %all_gather.19.gram_ref = f32[1280,128]{1,0:T(8,128)S(1)} all-gather(f32[160,128]{1,0:T(8,128)S(1)} %reduce_sum.19), channel_id=1, replica_groups=mesh['pipe'=4,'seq'=16,'tensor'=8] {'tensor'}, dimensions={0}, use_global_device_ids=true | all-gather | bytes 737280 | tf_op jit(solution)/shard_map/all_gather | solution.py:439
  170.0 13.5 %shard_map.80.part_ref = f32[512,512]{1,0:T(8,128)S(1)} custom-call(f32[1280,128]{1,0:T(8,128)S(1)} %all_gather.19.gram_ref), custom_call_target="tpu_custom_call" | custom-call | tf_op jit(solution)/shard_map/pallas_call | solution.py:388
  183.5 0.0 reduce-scatter.2.cloned.1.call-done
  183.6 3.9 %collective-permute-start.1 = (bf16[256,512]{1,0:T(8,128)(2,1)}, bf16[256,512]{1,0:T(8,128)(2,1)S(1)}, u32[]{:S(2)}, u32[]{:S(2)}) collective-permute-start(bf16[256,512]{1,0:T(8,128)(2,1)} %reduce-scatter.2.cloned.1.call-done), channel_id=1, source_target_pairs={{0,384},{128,0},{256,128},{384,256},{1,385},{129,1},{257,129},{385... | collective-permute-start | bytes 786440 | tf_op jit(solution)/shard_map/ppermute | solution.py:442
  187.5 6.5 %shard_map.81 = bf16[1024,512]{1,0:T(8,128)(2,1)} custom-call(f32[512,512]{1,0:T(8,128)S(1)} %shard_map.80.part_ref, f32[1024,512]{1,0:T(8,128)S(1)} %copy-done), custom_call_target="tpu_custom_call" | custom-call | tf_op jit(solution)/shard_map/pallas_call | solution.py:400
  194.1 0.7 copy.9
  (14 shorter events, 0.1 us)
Async XLA Ops:
  7.2 119.0 %all-gather.4.cloned.1.call-start = ((), (), s32[]{:S(2)}) async-start(), calls=%async_computation.5 | async-start | bytes 8912896 | tf_op jit(solution)/shard_map/all_gather | solution.py:426
  10.4 5.7 %collective-permute-start = (bf16[16,1024]{1,0:T(8,128)(2,1)S(1)}, bf16[16,1024]{1,0:T(8,128)(2,1)S(1)}, u32[]{:S(2)}, u32[]{:S(2)}) collective-permute-start(bf16[16,1024]{1,0:T(8,128)(2,1)S(1)} %pad_maximum_fusion), channel_id=1, source_target_pairs={{8,0},{16,8},{24,16},{32,24},{40,32},{48,40},{56,48},{64,56},{72,6... | collective-permute-start | bytes 98312 | tf_op jit(solution)/shard_map/ppermute | solution.py:420
  16.0 0.6 copy-start.3
  71.2 35.4 %all-to-all-start.1 = ((bf16[8,16,16,512]{3,2,1,0:T(8,128)(2,1)}), bf16[8,16,16,512]{3,2,1,0:T(8,128)(2,1)S(1)}, u32[]{:S(2)}, u32[]{:S(2)}) async-start(bf16[8,16,16,512]{3,2,1,0:T(8,128)(2,1)} %broadcast_in_dim.12), calls=%async_computation.1 | async-start | bytes 4194304 | tf_op jit(solution)/shard_map/all_to_all | solution.py:432
  80.3 103.3 %reduce-scatter.2.cloned.1.call-start = ((), (), s32[]{:S(2)}) async-start(), calls=%async_computation.4 | async-start | bytes 2359296 | tf_op jit(solution)/shard_map/reduce_scatter | solution.py:437
  106.6 19.5 %copy-start.1 = (bf16[8,16,16,512]{3,2,1,0:T(8,128)(2,1)}, bf16[8,16,16,512]{3,2,1,0:T(8,128)(2,1)S(1)}, u32[]{:S(2)}) copy-start(bf16[8,16,16,512]{3,2,1,0:T(8,128)(2,1)S(1)} %all-to-all-done.1.rows_ref) | copy-start | bytes 6291460
  138.6 1.1 copy-start.2
  139.6 47.9 %copy-start = (f32[1024,512]{1,0:T(8,128)S(1)}, f32[1024,512]{1,0:T(8,128)}, u32[]{:S(2)}) copy-start(f32[1024,512]{1,0:T(8,128)} %get-tuple-element.21.sketch_ref) | copy-start | bytes 6291460
  183.6 10.5 %collective-permute-start.1 = (bf16[256,512]{1,0:T(8,128)(2,1)}, bf16[256,512]{1,0:T(8,128)(2,1)S(1)}, u32[]{:S(2)}, u32[]{:S(2)}) collective-permute-start(bf16[256,512]{1,0:T(8,128)(2,1)} %reduce-scatter.2.cloned.1.call-done), channel_id=1, source_target_pairs={{0,384},{128,0},{256,128},{384,256},{1,385},{129,1},{257,129},{385... | collective-permute-start | bytes 786440 | tf_op jit(solution)/shard_map/ppermute | solution.py:442
Sparse Core Ops, SparseCore 0:
  10.7 115.4 all-gather.3
  138.7 38.6 reduce-scatter.1
